TPU v7x, 128 devices: a whole 4x4x4 slice. The times are simulated.
128 devices in a mesh: space: 128 (over x, y, z, core).
Axes of the slice: x: 4, y: 4, z: 4, core: 2. Of those that a mesh axis runs over, the one named last changes fastest.
Arguments:
- state: float32 [131072, 1024], P('space'), may hold values from -6 to 6
- obs_value: float32 [65536], P('space'), may hold values from -6 to 6
- obs_sigma: float32 [65536], P('space'), may hold values from 0.3 to 1.5
- obs_noise: float32 [65536, 1024], P('space'), may hold values from -6 to 6
- obs_pos: int32 [2, 65536], P(None, 'space'), may hold values from 0 to 511, as said below
- obs_side: int32 [65536], P('space'), may hold values from 0 to 1
Outputs:
- predicted_states: float32 [131072, 1024], P('space')
Inputs may be any that keep to these rules, and one draw needn't show every extreme that they name: `obs_pos`: observation o lies in grid row (o // 512) * 4 plus 0 to 3; its column is 0 to 255.
All inputs are finite; a program needn't handle non-finite values.
Results may differ from a plain program's by a relative error of at most 0.0038.
Values may be sent and summed in bfloat16 or wider, within the bound.
No kernel may reach another device: no remote copies, remote signals or barrier semaphores. Data moves between devices by JAX's collectives and lax.ppermute only.
A program may use at most 128 MiB of HBM per device.

v0:
```python
import functools

import jax
import jax.numpy as jnp
from jax import lax
from jax.experimental import pallas as pl
from jax.experimental.pallas import tpu as pltpu
from jax.sharding import PartitionSpec as P

WIDTH = 256
ROWS = 4
REACH = 4
CELLS = ROWS * WIDTH
OBS = 512
M = 1024
CHUNK = 16
VMEM = 48 * 1024 * 1024
F32 = jnp.float32
BF16 = jnp.bfloat16


def params():
    return pltpu.CompilerParams(vmem_limit_bytes=VMEM, dimension_semantics=("arbitrary",))


def cost(flops, nbytes):
    return pl.CostEstimate(flops=int(flops), bytes_accessed=int(nbytes), transcendentals=0)


def column(row):
    return jnp.broadcast_to(row, (8, row.shape[1])).T[:, 0:1]


def prep_kernel(row0_ref, state_ref, pos_ref, side_ref, x_ref, a_ref, dev_ref, mean_ref, hi_scr, lo_scr, m_scr):
    r = pl.program_id(0)
    s = state_ref[...]
    ms = jnp.mean(s, axis=1, keepdims=True)
    sd = s - ms
    x_ref[...] = sd.astype(BF16)
    dev = 0.5 * (sd + pltpu.roll(sd, WIDTH - 1, 0))
    hi = dev.astype(BF16)
    here = pl.ds(pl.multiple_of(r * WIDTH, WIDTH), WIDTH)
    hi_scr[here, :] = hi
    lo_scr[here, :] = (dev - hi.astype(F32)).astype(BF16)
    mw = jnp.broadcast_to(ms, (WIDTH, 128))
    pm = 0.5 * (mw + pltpu.roll(mw, WIDTH - 1, 0))
    p0 = pm.astype(BF16).astype(F32)
    p1 = (pm - p0).astype(BF16).astype(F32)
    p2 = pm - p0 - p1
    lane = lax.broadcasted_iota(jnp.int32, (WIDTH, 128), 1)
    m_scr[here, :] = jnp.where(
        lane == 0, p0, jnp.where(lane == 1, p1, jnp.where(lane == 2, p2, 0.0))
    ).astype(BF16)

    @pl.when(r == ROWS - 1)
    def _():
        local = pos_ref[0:1, :] - row0_ref[0]
        col = pos_ref[1:2, :]
        left = (col + side_ref[...] - 1) & (WIDTH - 1)
        index = column((local * WIDTH + left).astype(F32)).astype(jnp.int32)
        cells = lax.broadcasted_iota(jnp.int32, (OBS, CELLS), 1)
        pick = jnp.where(cells == index, 1.0, 0.0).astype(BF16)
        for n in range(4):
            part = slice(n * 256, (n + 1) * 256)
            high = jnp.dot(pick, hi_scr[:, part], preferred_element_type=F32)
            low = jnp.dot(pick, lo_scr[:, part], preferred_element_type=F32)
            a_ref[0:OBS, part] = high.astype(BF16)
            dev_ref[:, part] = high + low
        mg = jnp.dot(pick, m_scr[...], preferred_element_type=F32)
        mean_ref[...] = jnp.broadcast_to(jnp.sum(mg, axis=1, keepdims=True), (OBS, 128))
        sub = lax.broadcasted_iota(jnp.int32, (16, OBS), 0)
        code = jnp.where(sub == 0, local.astype(F32), jnp.where(sub == 1, col.astype(F32), 0.0))
        a_ref[OBS : OBS + 16, 0:OBS] = code.astype(BF16)
        a_ref[OBS : OBS + 16, OBS:M] = jnp.zeros((16, M - OBS), BF16)


def prep(row0, state, pos, side):
    full = lambda shape: pl.BlockSpec(shape, lambda r: (0,) * len(shape))
    return pl.pallas_call(
        prep_kernel,
        grid=(ROWS,),
        in_specs=[
            pl.BlockSpec(memory_space=pltpu.SMEM),
            pl.BlockSpec((WIDTH, M), lambda r: (r, 0)),
            full((2, OBS)),
            full((1, OBS)),
        ],
        out_specs=[
            pl.BlockSpec((WIDTH, M), lambda r: (r, 0)),
            full((OBS + 16, M)),
            full((OBS, M)),
            full((OBS, 128)),
        ],
        out_shape=[
            jax.ShapeDtypeStruct((CELLS, M), BF16),
            jax.ShapeDtypeStruct((OBS + 16, M), BF16),
            jax.ShapeDtypeStruct((OBS, M), F32),
            jax.ShapeDtypeStruct((OBS, 128), F32),
        ],
        scratch_shapes=[
            pltpu.VMEM((CELLS, M), BF16),
            pltpu.VMEM((CELLS, M), BF16),
            pltpu.VMEM((CELLS, 128), BF16),
        ],
        compiler_params=params(),
        cost_estimate=cost(4 * OBS * CELLS * M, 10 << 20),
        name="prep",
    )(row0, state, pos, side)


def weight_kernel(dev_ref, mean_ref, value_ref, sigma_ref, noise_ref, w_ref):
    dev = dev_ref[...]
    spread = jnp.sum(dev * dev, axis=1, keepdims=True) * (1.0 / (M - 1))
    value = column(value_ref[...])
    sigma = column(sigma_ref[...])
    scale = 1.0 / (spread + sigma * sigma)
    base = value - mean_ref[:, 0:1]
    w_ref[...] = ((base + sigma * noise_ref[...] - dev) * scale).astype(BF16)


def weigh(dev, mean, value, sigma, noise):
    rows = 128
    return pl.pallas_call(
        weight_kernel,
        grid=(OBS // rows,),
        in_specs=[
            pl.BlockSpec((rows, M), lambda i: (i, 0)),
            pl.BlockSpec((rows, 128), lambda i: (i, 0)),
            pl.BlockSpec((1, rows), lambda i: (0, i)),
            pl.BlockSpec((1, rows), lambda i: (0, i)),
            pl.BlockSpec((rows, M), lambda i: (i, 0)),
        ],
        out_specs=pl.BlockSpec((rows, M), lambda i: (i, 0)),
        out_shape=jax.ShapeDtypeStruct((OBS, M), BF16),
        compiler_params=params(),
        cost_estimate=cost(8 * OBS * M, 5 << 20),
        name="weigh",
    )(dev, mean, value, sigma, noise)


def gain_rows(r, x, a_ref, offset, cov_scr, put):
    cov_scr[...] = lax.dot_general(
        x, a_ref[0:OBS, :], (((1,), (1,)), ((), ())), preferred_element_type=F32
    )
    code = a_ref[OBS : OBS + 16, 0:OBS].astype(F32)
    gap = jnp.abs(code[0:1, :] + (ROWS * offset - r).astype(F32))
    row2 = jnp.where(gap > REACH * ROWS, 1e4, gap * gap * (1.0 / 256.0))
    col = code[1:2, :] * (1.0 / 16.0)
    n1 = 1.0 / (M - 1)
    for i in range(WIDTH // CHUNK):
        rows = slice(i * CHUNK, (i + 1) * CHUNK)
        q = (lax.broadcasted_iota(jnp.int32, (CHUNK, 1), 0) + i * CHUNK).astype(F32) * (1.0 / 16.0)
        d = jnp.abs(q - col)
        d = jnp.minimum(d, 16.0 - d)
        z2 = d * d + row2
        inv = lax.rsqrt(jnp.maximum(z2, 1e-9))
        z = z2 * inv
        near = z2 * (z * ((0.625 * n1) + z * ((0.5 * n1) - (0.25 * n1) * z)) - (5.0 / 3.0 * n1)) + n1
        u = jnp.maximum(2.0 - z, 0.0)
        u2 = u * u
        far = (u2 * u2) * (z2 + (2.0 * z - 0.5)) * (inv * (n1 / 12.0))
        put(rows, (jnp.where(z2 <= 1.0, near, far) * cov_scr[rows, :]).astype(BF16))


def contribute_kernel(offsets, first, *refs):
    n = len(offsets)
    x_ref = refs[0]
    a_refs = refs[1 : 1 + n]
    w_refs = refs[1 + n : 1 + 2 * n]
    acc_ref = refs[1 + 2 * n]
    out_ref, cov_scr, g_scr = refs[-3:]
    r = pl.program_id(0)
    x = x_ref[...]
    total = acc_ref[...]
    for k, offset in enumerate(offsets):

        def put(rows, val):
            g_scr[rows, :] = val

        gain_rows(r, x, a_refs[k], offset, cov_scr, put)
        total = total + jnp.dot(g_scr[...], w_refs[k][...], preferred_element_type=F32)
    out_ref[...] = total


def contribute(x, packets, weights, offsets, acc, first):
    n = len(offsets)
    tile = pl.BlockSpec((WIDTH, M), lambda r: (r, 0))
    whole = lambda rows: pl.BlockSpec((rows, M), lambda r: (0, 0))
    return pl.pallas_call(
        functools.partial(contribute_kernel, offsets, first),
        grid=(ROWS,),
        in_specs=[tile] + [whole(OBS + 16)] * n + [whole(OBS)] * n + [tile],
        out_specs=tile,
        out_shape=jax.ShapeDtypeStruct((CELLS, M), F32),
        scratch_shapes=[pltpu.VMEM((WIDTH, OBS), F32), pltpu.VMEM((WIDTH, OBS), BF16)],
        input_output_aliases={} if first else {1 + 2 * n: 0},
        compiler_params=params(),
        cost_estimate=cost(8 * n * CELLS * OBS * M, 10 << 20),
        name="contribute",
    )(x, *packets, *weights, acc)


def gain_kernel(offsets, x_ref, au_ref, ad_ref, g_ref, cov_scr):
    r = pl.program_id(0)
    x = x_ref[...]
    for k, (a_ref, offset) in enumerate(zip((au_ref, ad_ref), offsets)):

        def put(rows, val, k=k):
            g_ref[rows, k * OBS : (k + 1) * OBS] = val

        gain_rows(r, x, a_ref, offset, cov_scr, put)


def gains(x, packets, offsets):
    tile = pl.BlockSpec((WIDTH, M), lambda r: (r, 0))
    whole = pl.BlockSpec((OBS + 16, M), lambda r: (0, 0))
    return pl.pallas_call(
        functools.partial(gain_kernel, offsets),
        grid=(ROWS,),
        in_specs=[tile, whole, whole],
        out_specs=pl.BlockSpec((WIDTH, 2 * OBS), lambda r: (r, 0)),
        out_shape=jax.ShapeDtypeStruct((CELLS, 2 * OBS), BF16),
        scratch_shapes=[pltpu.VMEM((WIDTH, OBS), F32)],
        compiler_params=params(),
        cost_estimate=cost(8 * CELLS * OBS * M, 6 << 20),
        name="gains",
    )(x, *packets)


def edge_kernel(acc_ref, g_ref, wu_ref, wd_ref, out_ref, send_ref):
    total = acc_ref[...]
    total = total + jnp.dot(g_ref[:, 0:OBS], wu_ref[...], preferred_element_type=F32)
    total = total + jnp.dot(g_ref[:, OBS : 2 * OBS], wd_ref[...], preferred_element_type=F32)
    out_ref[...] = total
    send_ref[0] = total.astype(BF16)


def edges(acc, gain, wu, wd):
    tile = pl.BlockSpec((WIDTH, M), lambda i: (3 * i, 0))
    whole = pl.BlockSpec((OBS, M), lambda i: (0, 0))
    return pl.pallas_call(
        edge_kernel,
        grid=(2,),
        in_specs=[tile, tile, whole, whole],
        out_specs=[
            pl.BlockSpec((WIDTH, M), lambda i: (i, 0)),
            pl.BlockSpec((1, WIDTH, M), lambda i: (i, 0, 0)),
        ],
        out_shape=[
            jax.ShapeDtypeStruct((2 * WIDTH, M), F32),
            jax.ShapeDtypeStruct((2, WIDTH, M), BF16),
        ],
        compiler_params=params(),
        cost_estimate=cost(4 * CELLS * OBS * M, 6 << 20),
        name="edges",
    )(acc, gain, wu, wd)


def advance(a, above, below):
    right = pltpu.roll(a, WIDTH - 1, 0)
    left = pltpu.roll(a, 1, 0)
    pull = 0.05 * a * (above - below + (right - left))
    spread = 0.2 * (above + below + right + left - 4.0 * a)
    return a - pull + spread


def inner_kernel(acc_ref, g_ref, wu_ref, wd_ref, edge_ref, mid_ref, out_ref):
    i = pl.program_id(0)
    lanes = pl.ds(pl.multiple_of(i * 256, 256), 256)
    total = acc_ref[WIDTH : 3 * WIDTH, :]
    total = total + jnp.dot(
        g_ref[WIDTH : 3 * WIDTH, 0:OBS], wu_ref[...], preferred_element_type=F32
    )
    total = total + jnp.dot(
        g_ref[WIDTH : 3 * WIDTH, OBS : 2 * OBS], wd_ref[...], preferred_element_type=F32
    )
    mid_ref[...] = total
    one = total[0:WIDTH]
    two = total[WIDTH : 2 * WIDTH]
    out_ref[0:WIDTH, :] = advance(one, two, edge_ref[0:WIDTH, :])
    out_ref[WIDTH : 2 * WIDTH, :] = advance(two, edge_ref[WIDTH : 2 * WIDTH, :], one)


def inner(acc, gain, wu, wd, edge):
    cols = lambda rows: pl.BlockSpec((rows, 256), lambda i: (0, i))
    return pl.pallas_call(
        inner_kernel,
        grid=(M // 256,),
        in_specs=[
            cols(CELLS),
            pl.BlockSpec((CELLS, 2 * OBS), lambda i: (0, 0)),
            cols(OBS),
            cols(OBS),
            cols(2 * WIDTH),
        ],
        out_specs=[cols(2 * WIDTH), cols(2 * WIDTH)],
        out_shape=[
            jax.ShapeDtypeStruct((2 * WIDTH, M), F32),
            jax.ShapeDtypeStruct((2 * WIDTH, M), F32),
        ],
        compiler_params=params(),
        cost_estimate=cost(4 * CELLS * OBS * M, 10 << 20),
        name="inner",
    )(acc, gain, wu, wd, edge)


def outer_kernel(edge_ref, mid_ref, before_ref, after_ref, pred_ref, out_ref):
    first = edge_ref[0:WIDTH, :]
    last = edge_ref[WIDTH : 2 * WIDTH, :]
    one = mid_ref[0:WIDTH, :]
    two = mid_ref[WIDTH : 2 * WIDTH, :]
    out_ref[0:WIDTH, :] = advance(first, one, before_ref[0].astype(F32))
    out_ref[WIDTH : 3 * WIDTH, :] = pred_ref[...]
    out_ref[3 * WIDTH : 4 * WIDTH, :] = advance(last, after_ref[0].astype(F32), two)


def outer(edge, mid, before, after, pred):
    cols = lambda rows: pl.BlockSpec((rows, 256), lambda i: (0, i))
    halo = pl.BlockSpec((1, WIDTH, 256), lambda i: (0, 0, i))
    return pl.pallas_call(
        outer_kernel,
        grid=(M // 256,),
        in_specs=[cols(2 * WIDTH), cols(2 * WIDTH), halo, halo, cols(2 * WIDTH)],
        out_specs=cols(CELLS),
        out_shape=jax.ShapeDtypeStruct((CELLS, M), F32),
        compiler_params=params(),
        cost_estimate=cost(20 * CELLS * M, 12 << 20),
        name="outer",
    )(edge, mid, before, after, pred)


def on_device(state, obs_value, obs_sigma, obs_noise, obs_pos, obs_side):
    device = lax.axis_index("space")
    slabs = lax.axis_size("space")
    up = [(i, (i + 1) % slabs) for i in range(slabs)]
    down = [(j, i) for i, j in up]
    row0 = (device * ROWS).astype(jnp.int32).reshape(1)
    x, a, dev, mean = prep(row0, state, obs_pos, obs_side.reshape(1, OBS))
    w = weigh(dev, mean, obs_value.reshape(1, OBS), obs_sigma.reshape(1, OBS), obs_noise)
    acc = contribute(x, (a,), (w,), (0,), state, True)
    lower_a = upper_a = a
    lower_w = upper_w = w
    for step in range(1, REACH + 1):
        lower_a = lax.ppermute(lower_a, "space", up)
        upper_a = lax.ppermute(upper_a, "space", down)
        lower_w = lax.ppermute(lower_w, "space", up)
        upper_w = lax.ppermute(upper_w, "space", down)
        if step < REACH:
            acc = contribute(
                x, (lower_a, upper_a), (lower_w, upper_w), (-step, step), acc, False
            )
    gain = gains(x, (lower_a, upper_a), (-REACH, REACH))
    edge, send = edges(acc, gain, lower_w, upper_w)
    before = lax.ppermute(send[1:2], "space", up)
    after = lax.ppermute(send[0:1], "space", down)
    mid, pred = inner(acc, gain, lower_w, upper_w, edge)
    return outer(edge, mid, before, after, pred)


def solution(mesh):
    placed = (
        P("space", None),
        P("space"),
        P("space"),
        P("space", None),
        P(None, "space"),
        P("space"),
    )
    return jax.shard_map(
        on_device, mesh=mesh, in_specs=placed, out_specs=P("space", None), check_vma=False
    )
```

profile of v0, /device:TPU:0, one launch (start us, length us, event | category | flops | bytes accessed | tf_op | source)
XLA Modules:
  0.0 152.4 jit_solution(16163536684702400655)
XLA Ops:
  0.0 0.7 copy-done.6
  0.7 0.7 copy-done.7
  1.4 7.3 %prep.1 = (bf16[1024,1024]{1,0:T(8,128)(2,1)S(1)}, bf16[528,1024]{1,0:T(8,128)(2,1)S(1)}, f32[512,1024]{1,0:T(8,128)S(1)}, f32[512,128]{1,0:T(8,128)S(1)}) custom-call(s32[1]{0:T(128)} %bitcast.row0_ref, f32[1024,1024]{1,0:T(8,128)} %refs_3_.1, s32[2,512]{1,0:T(2,128)S(1)} %copy-done.6, s32[1,512]{1,0:T(1,128)S(1)} %bitcast.6), custom_call_target="tpu_custom_call" | custom-call | flops 2147483648 | bytes 10485760 | tf_op jit(solution)/shard_map/prep/pallas_call | solution.py:79
  8.7 0.1 collective-permute-start
  8.8 8.3 %collective-permute-start.3 = (bf16[528,1024]{1,0:T(8,128)(2,1)S(1)}, bf16[528,1024]{1,0:T(8,128)(2,1)S(1)}, u32[]{:S(2)}, u32[]{:S(2)}) collective-permute-start(bf16[528,1024]{1,0:T(8,128)(2,1)S(1)} %get-tuple-element.14.refs_1_), channel_id=1, source_target_pairs={{1,0},{2,1},{3,2},{4,3},{5,4},{6,5},{7,6},{8,7},{9,8},{10,9},{11,1... | collective-permute-start | bytes 3244040 | tf_op jit(solution)/shard_map/ppermute | solution.py:345
  17.1 1.3 weigh.1.refs_2_
  18.3 0.7 collective-permute-start.9
  19.1 0.0 collective-permute-start.6
  19.1 10.7 %collective-permute-done.refs_1_ = bf16[528,1024]{1,0:T(8,128)(2,1)S(1)} collective-permute-done((bf16[528,1024]{1,0:T(8,128)(2,1)S(1)}, bf16[528,1024]{1,0:T(8,128)(2,1)S(1)}, u32[]{:S(2)}, u32[]{:S(2)}) %collective-permute-start) | collective-permute-done | bytes 1081376 | tf_op jit(solution)/shard_map/ppermute | solution.py:344
  29.8 0.0 collective-permute-start.1
  29.8 0.0 collective-permute-done.3.refs_2_
  29.8 7.2 %collective-permute-start.4 = (bf16[528,1024]{1,0:T(8,128)(2,1)S(1)}, bf16[528,1024]{1,0:T(8,128)(2,1)S(1)}, u32[]{:S(2)}, u32[]{:S(2)}) collective-permute-start(bf16[528,1024]{1,0:T(8,128)(2,1)S(1)} %collective-permute-done.3.refs_2_), channel_id=1, source_target_pairs={{1,0},{2,1},{3,2},{4,3},{5,4},{6,5},{7,6},{8,7},{9,8},{10,9},{11,1... | collective-permute-start | bytes 3244040 | tf_op jit(solution)/shard_map/ppermute | solution.py:345
  37.1 3.9 %collective-permute-done.9.refs_4_ = bf16[512,1024]{1,0:T(8,128)(2,1)S(1)} collective-permute-done((bf16[512,1024]{1,0:T(8,128)(2,1)S(1)}, bf16[512,1024]{1,0:T(8,128)(2,1)S(1)}, u32[]{:S(2)}, u32[]{:S(2)}) %collective-permute-start.9) | collective-permute-done | bytes 1048608 | tf_op jit(solution)/shard_map/ppermute | solution.py:347
  41.0 7.3 %collective-permute-start.10 = (bf16[512,1024]{1,0:T(8,128)(2,1)S(1)}, bf16[512,1024]{1,0:T(8,128)(2,1)S(1)}, u32[]{:S(2)}, u32[]{:S(2)}) collective-permute-start(bf16[512,1024]{1,0:T(8,128)(2,1)S(1)} %collective-permute-done.9.refs_4_), channel_id=1, source_target_pairs={{1,0},{2,1},{3,2},{4,3},{5,4},{6,5},{7,6},{8,7},{9,8},{10,9},{11,1... | collective-permute-start | bytes 3145736 | tf_op jit(solution)/shard_map/ppermute | solution.py:347
  48.3 4.3 %collective-permute-done.1.refs_1_ = bf16[528,1024]{1,0:T(8,128)(2,1)S(1)} collective-permute-done((bf16[528,1024]{1,0:T(8,128)(2,1)S(1)}, bf16[528,1024]{1,0:T(8,128)(2,1)S(1)}, u32[]{:S(2)}, u32[]{:S(2)}) %collective-permute-start.1) | collective-permute-done | bytes 1081376 | tf_op jit(solution)/shard_map/ppermute | solution.py:344
  52.6 7.2 %collective-permute-start.5 = (bf16[528,1024]{1,0:T(8,128)(2,1)S(1)}, bf16[528,1024]{1,0:T(8,128)(2,1)S(1)}, u32[]{:S(2)}, u32[]{:S(2)}) collective-permute-start(bf16[528,1024]{1,0:T(8,128)(2,1)S(1)} %collective-permute-done.4.refs_2_), channel_id=1, source_target_pairs={{1,0},{2,1},{3,2},{4,3},{5,4},{6,5},{7,6},{8,7},{9,8},{10,9},{11,1... | collective-permute-start | bytes 3244040 | tf_op jit(solution)/shard_map/ppermute | solution.py:345
  59.9 7.6 %contribute.4.refs_5_ = f32[1024,1024]{1,0:T(8,128)} custom-call(bf16[1024,1024]{1,0:T(8,128)(2,1)S(1)} %get-tuple-element.13.refs_0_.x_ref, bf16[528,1024]{1,0:T(8,128)(2,1)S(1)} %get-tuple-element.14.refs_1_, bf16[512,1024]{1,0:T(8,128)(2,1)S(1)} %weigh.1.refs_2_, f32[1024,1024]{1,0:T(8,128)} %refs_3_.1), custom_call_target="tpu_custom_call" | custom-call | flops 4294967296 | bytes 10485760 | tf_op jit(solution)/shard_map/contribute/pallas_call | solution.py:189
  67.4 3.7 %collective-permute-start.11 = (bf16[512,1024]{1,0:T(8,128)(2,1)S(1)}, bf16[512,1024]{1,0:T(8,128)(2,1)S(1)}, u32[]{:S(2)}, u32[]{:S(2)}) collective-permute-start(bf16[512,1024]{1,0:T(8,128)(2,1)S(1)} %collective-permute-done.10.refs_4_), channel_id=1, source_target_pairs={{1,0},{2,1},{3,2},{4,3},{5,4},{6,5},{7,6},{8,7},{9,8},{10,9},{11,1... | collective-permute-start | bytes 3145736 | tf_op jit(solution)/shard_map/ppermute | solution.py:347
  71.1 11.3 %contribute.5.refs_5_ = f32[1024,1024]{1,0:T(8,128)} custom-call(bf16[1024,1024]{1,0:T(8,128)(2,1)} %copy-done.8, bf16[528,1024]{1,0:T(8,128)(2,1)S(1)} %collective-permute-done.refs_1_, bf16[528,1024]{1,0:T(8,128)(2,1)S(1)} %collective-permute-done.3.refs_2_, bf16[512,1024]{1,0:T(8,128)(2,1)S(1)} %collective-permute-done.6.refs_3_, ...), custom_call_target="tpu_custom_call", output_to_operand_aliasing={{}: (5, {})} | custom-call | flops 8589934592 | bytes 10485760 | tf_op jit(solution)/shard_map/contribute/pallas_call | solution.py:189
  82.5 7.4 %collective-permute-start.13 = (bf16[528,1024]{1,0:T(8,128)(2,1)S(1)}, bf16[528,1024]{1,0:T(8,128)(2,1)S(1)}, u32[]{:S(2)}, u32[]{:S(2)}) collective-permute-start(bf16[528,1024]{1,0:T(8,128)(2,1)S(1)} %collective-permute-done.5.refs_2_), channel_id=1, source_target_pairs={{1,0},{2,1},{3,2},{4,3},{5,4},{6,5},{7,6},{8,7},{9,8},{10,9},{11,1... | collective-permute-start | bytes 3244040 | tf_op jit(solution)/shard_map/ppermute | solution.py:345
  89.9 11.3 %contribute.6.refs_5_ = f32[1024,1024]{1,0:T(8,128)} custom-call(bf16[1024,1024]{1,0:T(8,128)(2,1)} %copy-done.8, bf16[528,1024]{1,0:T(8,128)(2,1)S(1)} %collective-permute-done.1.refs_1_, bf16[528,1024]{1,0:T(8,128)(2,1)S(1)} %collective-permute-done.4.refs_2_, ...), custom_call_target="tpu_custom_call", output_to_operand_aliasing={{}: (5, {})} | custom-call | flops 8589934592 | bytes 10485760 | tf_op jit(solution)/shard_map/contribute/pallas_call | solution.py:189
  101.2 7.2 %collective-permute-start.15 = (bf16[512,1024]{1,0:T(8,128)(2,1)S(1)}, bf16[512,1024]{1,0:T(8,128)(2,1)S(1)}, u32[]{:S(2)}, u32[]{:S(2)}) collective-permute-start(bf16[512,1024]{1,0:T(8,128)(2,1)S(1)} %collective-permute-done.11.refs_4_), channel_id=1, source_target_pairs={{1,0},{2,1},{3,2},{4,3},{5,4},{6,5},{7,6},{8,7},{9,8},{10,9},{11,1... | collective-permute-start | bytes 3145736 | tf_op jit(solution)/shard_map/ppermute | solution.py:347
  108.4 11.8 %contribute.7.acc_ref = f32[1024,1024]{1,0:T(8,128)} custom-call(bf16[1024,1024]{1,0:T(8,128)(2,1)} %copy-done.8, bf16[528,1024]{1,0:T(8,128)(2,1)S(1)} %collective-permute-done.2.refs_1_, bf16[528,1024]{1,0:T(8,128)(2,1)S(1)} %collective-permute-done.5.refs_2_, bf16[512,1024]{1,0:T(8,128)(2,1)} %collective-permute-done.8.refs_3_, ...), custom_call_target="tpu_custom_call", output_to_operand_aliasing={{}: (5, {})} | custom-call | flops 8589934592 | bytes 10485760 | tf_op jit(solution)/shard_map/contribute/pallas_call | solution.py:189
  120.2 7.4 %gains.1.g_ref = bf16[1024,1024]{1,0:T(8,128)(2,1)S(1)} custom-call(bf16[1024,1024]{1,0:T(8,128)(2,1)} %copy-done.8, bf16[528,1024]{1,0:T(8,128)(2,1)S(1)} %collective-permute-done.12.au_ref, bf16[528,1024]{1,0:T(8,128)(2,1)S(1)} %collective-permute-done.13.ad_ref), custom_call_target="tpu_custom_call" | custom-call | flops 4294967296 | bytes 6291456 | tf_op jit(solution)/shard_map/gains/pallas_call | solution.py:217
  127.6 1.3 copy-done
  129.0 2.8 %edges.1 = (f32[512,1024]{1,0:T(8,128)S(1)}, bf16[2,256,1024]{2,1,0:T(8,128)(2,1)S(1)}) custom-call(f32[1024,1024]{1,0:T(8,128)} %contribute.7.acc_ref, bf16[1024,1024]{1,0:T(8,128)(2,1)} %copy-done, bf16[512,1024]{1,0:T(8,128)(2,1)S(1)} %collective-permute-done.14.wu_ref, bf16[512,1024]{1,0:T(8,128)(2,1)S(1)} %collective-permute-done.15.wd_ref), custom_call_target="tpu_custom_call" | custom-call | flops 2147483648 | bytes 6291456 | tf_op jit(solution)/shard_map/edges/pallas_call | solution.py:241
  131.8 1.3 copy-done.1
  133.1 0.1 fusion
  133.2 0.1 collective-permute-start.16
  133.2 7.2 %collective-permute-start.17 = (bf16[1,256,1024]{2,1,0:T(8,128)(2,1)S(1)}, bf16[1,256,1024]{2,1,0:T(8,128)(2,1)S(1)}, u32[]{:S(2)}, u32[]{:S(2)}) collective-permute-start(bf16[1,256,1024]{2,1,0:T(8,128)(2,1)S(1)} %get-tuple-element.21), channel_id=1, source_target_pairs={{1,0},{2,1},{3,2},{4,3},{5,4},{6,5},{7,6},{8,7},{9,8},{10,9},{11,1... | collective-permute-start | bytes 1572872 | tf_op jit(solution)/shard_map/ppermute | solution.py:355
  140.4 7.0 %inner.1 = (f32[512,1024]{1,0:T(8,128)S(1)}, f32[512,1024]{1,0:T(8,128)}) custom-call(f32[1024,1024]{1,0:T(8,128)} %contribute.7.acc_ref, bf16[1024,1024]{1,0:T(8,128)(2,1)} %copy-done, bf16[512,1024]{1,0:T(8,128)(2,1)S(1)} %collective-permute-done.14.wu_ref, bf16[512,1024]{1,0:T(8,128)(2,1)S(1)} %collective-permute-done.15.wd_ref, f32[512,1024]{1,0:T(8,128)} %copy-done.1), custom_call_target="tpu_custom_call" | custom-call | flops 2147483648 | bytes 10485760 | tf_op jit(solution)/shard_map/inner/pallas_call | solution.py:286
  147.5 4.9 %outer.1 = f32[1024,1024]{1,0:T(8,128)} custom-call(f32[512,1024]{1,0:T(8,128)S(1)} %copy-done.2, f32[512,1024]{1,0:T(8,128)S(1)} %get-tuple-element.18.mid_ref, bf16[1,256,1024]{2,1,0:T(8,128)(2,1)S(1)} %collective-permute-done.16.before_ref, bf16[1,256,1024]{2,1,0:T(8,128)(2,1)S(1)} %collective-permute-done.17.after_ref, ...), custom_call_target="tpu_custom_call" | custom-call | flops 20971520 | bytes 12582912 | tf_op jit(solution)/shard_map/outer/pallas_call | solution.py:320
  (33 shorter events, 0.1 us)
Async XLA Ops:
  0.0 0.7 copy-start.6
  0.7 0.7 copy-start.7
  1.4 15.7 %copy-start.3 = (f32[512,1024]{1,0:T(8,128)S(1)}, f32[512,1024]{1,0:T(8,128)}, u32[]{:S(2)}) copy-start(f32[512,1024]{1,0:T(8,128)} %noise_ref.1) | copy-start | bytes 6291460
  1.4 15.7 %copy-start.4 = (f32[512]{0:T(512)S(1)}, f32[512]{0:T(512)}, u32[]{:S(2)}) copy-start(f32[512]{0:T(512)} %param.7) | copy-start | bytes 6148
  1.4 15.7 %copy-start.5 = (f32[512]{0:T(512)S(1)}, f32[512]{0:T(512)}, u32[]{:S(2)}) copy-start(f32[512]{0:T(512)} %param.8) | copy-start | bytes 6148
  8.7 51.2 %copy-start.8 = (bf16[1024,1024]{1,0:T(8,128)(2,1)}, bf16[1024,1024]{1,0:T(8,128)(2,1)S(1)}, u32[]{:S(2)}) copy-start(bf16[1024,1024]{1,0:T(8,128)(2,1)S(1)} %get-tuple-element.13.refs_0_.x_ref) | copy-start | bytes 6291460
  8.7 21.1 %collective-permute-start = (bf16[528,1024]{1,0:T(8,128)(2,1)S(1)}, bf16[528,1024]{1,0:T(8,128)(2,1)S(1)}, u32[]{:S(2)}, u32[]{:S(2)}) collective-permute-start(bf16[528,1024]{1,0:T(8,128)(2,1)S(1)} %get-tuple-element.14.refs_1_), channel_id=1, source_target_pairs={{0,1},{1,2},{2,3},{3,4},{4,5},{5,6},{6,7},{7,8},{8,9},{9,10},{10,1... | collective-permute-start | bytes 3244040 | tf_op jit(solution)/shard_map/ppermute | solution.py:344
  8.8 21.0 %collective-permute-start.3 = (bf16[528,1024]{1,0:T(8,128)(2,1)S(1)}, bf16[528,1024]{1,0:T(8,128)(2,1)S(1)}, u32[]{:S(2)}, u32[]{:S(2)}) collective-permute-start(bf16[528,1024]{1,0:T(8,128)(2,1)S(1)} %get-tuple-element.14.refs_1_), channel_id=1, source_target_pairs={{1,0},{2,1},{3,2},{4,3},{5,4},{6,5},{7,6},{8,7},{9,8},{10,9},{11,1... | collective-permute-start | bytes 3244040 | tf_op jit(solution)/shard_map/ppermute | solution.py:345
  18.3 22.6 %collective-permute-start.9 = (bf16[512,1024]{1,0:T(8,128)(2,1)S(1)}, bf16[512,1024]{1,0:T(8,128)(2,1)S(1)}, u32[]{:S(2)}, u32[]{:S(2)}) collective-permute-start(bf16[512,1024]{1,0:T(8,128)(2,1)S(1)} %weigh.1.refs_2_), channel_id=1, source_target_pairs={{1,0},{2,1},{3,2},{4,3},{5,4},{6,5},{7,6},{8,7},{9,8},{10,9},{11,1... | collective-permute-start | bytes 3145736 | tf_op jit(solution)/shard_map/ppermute | solution.py:347
  19.1 29.2 %collective-permute-start.6 = (bf16[512,1024]{1,0:T(8,128)(2,1)S(1)}, bf16[512,1024]{1,0:T(8,128)(2,1)S(1)}, u32[]{:S(2)}, u32[]{:S(2)}) collective-permute-start(bf16[512,1024]{1,0:T(8,128)(2,1)S(1)} %weigh.1.refs_2_), channel_id=1, source_target_pairs={{0,1},{1,2},{2,3},{3,4},{4,5},{5,6},{6,7},{7,8},{8,9},{9,10},{10,1... | collective-permute-start | bytes 3145736 | tf_op jit(solution)/shard_map/ppermute | solution.py:346
  29.8 22.8 %collective-permute-start.1 = (bf16[528,1024]{1,0:T(8,128)(2,1)S(1)}, bf16[528,1024]{1,0:T(8,128)(2,1)S(1)}, u32[]{:S(2)}, u32[]{:S(2)}) collective-permute-start(bf16[528,1024]{1,0:T(8,128)(2,1)S(1)} %collective-permute-done.refs_1_), channel_id=1, source_target_pairs={{0,1},{1,2},{2,3},{3,4},{4,5},{5,6},{6,7},{7,8},{8,9},{9,10},{10,1... | collective-permute-start | bytes 3244040 | tf_op jit(solution)/shard_map/ppermute | solution.py:344
  29.8 22.8 %collective-permute-start.4 = (bf16[528,1024]{1,0:T(8,128)(2,1)S(1)}, bf16[528,1024]{1,0:T(8,128)(2,1)S(1)}, u32[]{:S(2)}, u32[]{:S(2)}) collective-permute-start(bf16[528,1024]{1,0:T(8,128)(2,1)S(1)} %collective-permute-done.3.refs_2_), channel_id=1, source_target_pairs={{1,0},{2,1},{3,2},{4,3},{5,4},{6,5},{7,6},{8,7},{9,8},{10,9},{11,1... | collective-permute-start | bytes 3244040 | tf_op jit(solution)/shard_map/ppermute | solution.py:345
  41.0 26.5 %collective-permute-start.10 = (bf16[512,1024]{1,0:T(8,128)(2,1)S(1)}, bf16[512,1024]{1,0:T(8,128)(2,1)S(1)}, u32[]{:S(2)}, u32[]{:S(2)}) collective-permute-start(bf16[512,1024]{1,0:T(8,128)(2,1)S(1)} %collective-permute-done.9.refs_4_), channel_id=1, source_target_pairs={{1,0},{2,1},{3,2},{4,3},{5,4},{6,5},{7,6},{8,7},{9,8},{10,9},{11,1... | collective-permute-start | bytes 3145736 | tf_op jit(solution)/shard_map/ppermute | solution.py:347
  48.3 22.8 %collective-permute-start.7 = (bf16[512,1024]{1,0:T(8,128)(2,1)S(1)}, bf16[512,1024]{1,0:T(8,128)(2,1)S(1)}, u32[]{:S(2)}, u32[]{:S(2)}) collective-permute-start(bf16[512,1024]{1,0:T(8,128)(2,1)S(1)} %collective-permute-done.6.refs_3_), channel_id=1, source_target_pairs={{0,1},{1,2},{2,3},{3,4},{4,5},{5,6},{6,7},{7,8},{8,9},{9,10},{10,1... | collective-permute-start | bytes 3145736 | tf_op jit(solution)/shard_map/ppermute | solution.py:346
  52.6 29.8 %collective-permute-start.2 = (bf16[528,1024]{1,0:T(8,128)(2,1)S(1)}, bf16[528,1024]{1,0:T(8,128)(2,1)S(1)}, u32[]{:S(2)}, u32[]{:S(2)}) collective-permute-start(bf16[528,1024]{1,0:T(8,128)(2,1)S(1)} %collective-permute-done.1.refs_1_), channel_id=1, source_target_pairs={{0,1},{1,2},{2,3},{3,4},{4,5},{5,6},{6,7},{7,8},{8,9},{9,10},{10,1... | collective-permute-start | bytes 3244040 | tf_op jit(solution)/shard_map/ppermute | solution.py:344
  52.6 29.8 %collective-permute-start.5 = (bf16[528,1024]{1,0:T(8,128)(2,1)S(1)}, bf16[528,1024]{1,0:T(8,128)(2,1)S(1)}, u32[]{:S(2)}, u32[]{:S(2)}) collective-permute-start(bf16[528,1024]{1,0:T(8,128)(2,1)S(1)} %collective-permute-done.4.refs_2_), channel_id=1, source_target_pairs={{1,0},{2,1},{3,2},{4,3},{5,4},{6,5},{7,6},{8,7},{9,8},{10,9},{11,1... | collective-permute-start | bytes 3244040 | tf_op jit(solution)/shard_map/ppermute | solution.py:345
  67.4 33.8 %collective-permute-start.11 = (bf16[512,1024]{1,0:T(8,128)(2,1)S(1)}, bf16[512,1024]{1,0:T(8,128)(2,1)S(1)}, u32[]{:S(2)}, u32[]{:S(2)}) collective-permute-start(bf16[512,1024]{1,0:T(8,128)(2,1)S(1)} %collective-permute-done.10.refs_4_), channel_id=1, source_target_pairs={{1,0},{2,1},{3,2},{4,3},{5,4},{6,5},{7,6},{8,7},{9,8},{10,9},{11,1... | collective-permute-start | bytes 3145736 | tf_op jit(solution)/shard_map/ppermute | solution.py:347
  71.1 30.1 %collective-permute-start.8 = (bf16[512,1024]{1,0:T(8,128)(2,1)S(1)}, bf16[512,1024]{1,0:T(8,128)(2,1)}, u32[]{:S(2)}, u32[]{:S(2)}) collective-permute-start(bf16[512,1024]{1,0:T(8,128)(2,1)S(1)} %collective-permute-done.7.refs_3_), channel_id=1, source_target_pairs={{0,1},{1,2},{2,3},{3,4},{4,5},{5,6},{6,7},{7,8},{8,9},{9,10},{10,1... | collective-permute-start | bytes 3145736 | tf_op jit(solution)/shard_map/ppermute | solution.py:346
  82.5 37.7 %collective-permute-start.12 = (bf16[528,1024]{1,0:T(8,128)(2,1)S(1)}, bf16[528,1024]{1,0:T(8,128)(2,1)S(1)}, u32[]{:S(2)}, u32[]{:S(2)}) collective-permute-start(bf16[528,1024]{1,0:T(8,128)(2,1)S(1)} %collective-permute-done.2.refs_1_), channel_id=1, source_target_pairs={{0,1},{1,2},{2,3},{3,4},{4,5},{5,6},{6,7},{7,8},{8,9},{9,10},{10,1... | collective-permute-start | bytes 3244040 | tf_op jit(solution)/shard_map/ppermute | solution.py:344
  82.5 37.7 %collective-permute-start.13 = (bf16[528,1024]{1,0:T(8,128)(2,1)S(1)}, bf16[528,1024]{1,0:T(8,128)(2,1)S(1)}, u32[]{:S(2)}, u32[]{:S(2)}) collective-permute-start(bf16[528,1024]{1,0:T(8,128)(2,1)S(1)} %collective-permute-done.5.refs_2_), channel_id=1, source_target_pairs={{1,0},{2,1},{3,2},{4,3},{5,4},{6,5},{7,6},{8,7},{9,8},{10,9},{11,1... | collective-permute-start | bytes 3244040 | tf_op jit(solution)/shard_map/ppermute | solution.py:345
  101.2 27.8 %collective-permute-start.14 = (bf16[512,1024]{1,0:T(8,128)(2,1)}, bf16[512,1024]{1,0:T(8,128)(2,1)S(1)}, u32[]{:S(2)}, u32[]{:S(2)}) collective-permute-start(bf16[512,1024]{1,0:T(8,128)(2,1)} %collective-permute-done.8.refs_3_), channel_id=1, source_target_pairs={{0,1},{1,2},{2,3},{3,4},{4,5},{5,6},{6,7},{7,8},{8,9},{9,10},{10,1... | collective-permute-start | bytes 3145736 | tf_op jit(solution)/shard_map/ppermute | solution.py:346
  101.2 27.7 %collective-permute-start.15 = (bf16[512,1024]{1,0:T(8,128)(2,1)S(1)}, bf16[512,1024]{1,0:T(8,128)(2,1)S(1)}, u32[]{:S(2)}, u32[]{:S(2)}) collective-permute-start(bf16[512,1024]{1,0:T(8,128)(2,1)S(1)} %collective-permute-done.11.refs_4_), channel_id=1, source_target_pairs={{1,0},{2,1},{3,2},{4,3},{5,4},{6,5},{7,6},{8,7},{9,8},{10,9},{11,1... | collective-permute-start | bytes 3145736 | tf_op jit(solution)/shard_map/ppermute | solution.py:347
  127.6 1.4 copy-start
  131.8 1.3 copy-start.1
  133.2 14.3 %collective-permute-start.16 = (bf16[1,256,1024]{2,1,0:T(8,128)(2,1)S(1)}, bf16[1,256,1024]{2,1,0:T(8,128)(2,1)S(1)}, u32[]{:S(2)}, u32[]{:S(2)}) collective-permute-start(bf16[1,256,1024]{2,1,0:T(8,128)(2,1)S(1)} %get-tuple-element.22), channel_id=1, source_target_pairs={{0,1},{1,2},{2,3},{3,4},{4,5},{5,6},{6,7},{7,8},{8,9},{9,10},{10,1... | collective-permute-start | bytes 1572872 | tf_op jit(solution)/shard_map/ppermute | solution.py:354
  133.2 14.2 %collective-permute-start.17 = (bf16[1,256,1024]{2,1,0:T(8,128)(2,1)S(1)}, bf16[1,256,1024]{2,1,0:T(8,128)(2,1)S(1)}, u32[]{:S(2)}, u32[]{:S(2)}) collective-permute-start(bf16[1,256,1024]{2,1,0:T(8,128)(2,1)S(1)} %get-tuple-element.21), channel_id=1, source_target_pairs={{1,0},{2,1},{3,2},{4,3},{5,4},{6,5},{7,6},{8,7},{9,8},{10,9},{11,1... | collective-permute-start | bytes 1572872 | tf_op jit(solution)/shard_map/ppermute | solution.py:355
  140.4 7.1 %copy-start.2 = (f32[512,1024]{1,0:T(8,128)S(1)}, f32[512,1024]{1,0:T(8,128)}, u32[]{:S(2)}) copy-start(f32[512,1024]{1,0:T(8,128)} %copy-done.1) | copy-start | bytes 6291460
where the time goes:
time: 153 us; the launch traced here: 152 us
  Pallas kernels  72.7 us (48%)
  starting transfers between devices  56.4 us (37%)
  waiting for transfers between devices  19 us (12%)
  local copies, waits for them, and re-layouts  4.09 us (3%)
    pallas_call x4, Pallas kernels, contribute(): pl.pallas_call(functools.partial(contribute_kernel, offsets, first), grid...  42 us
    ppermute x4, starting transfers between devices, on_device(): upper_a = lax.ppermute(upper_a, 'space', down)  30.2 us
    ppermute x4, starting transfers between devices, on_device(): upper_w = lax.ppermute(upper_w, 'space', down)  18.9 us
    ppermute x4, waiting for transfers between devices, on_device(): lower_a = lax.ppermute(lower_a, 'space', up)  15.1 us
    pallas_call x1, Pallas kernels, gains(): pl.pallas_call(functools.partial(gain_kernel, offsets), grid=(ROWS,), in_...  7.38 us
    pallas_call x1, Pallas kernels, prep(): pl.pallas_call(prep_kernel, grid=(ROWS,), in_specs=[pl.BlockSpec(memory_s...  7.31 us
    ppermute x1, starting transfers between devices, on_device(): after = lax.ppermute(send[0:1], 'space', down)  7.16 us
    pallas_call x1, Pallas kernels, inner(): pl.pallas_call(inner_kernel, grid=(M // 256,), in_specs=[cols(CELLS), pl....  7.04 us
  transfers between devices with their start and end apart: 18, of which 3 were waited for; matrix products, arithmetic and copies ran while one was open for 0% of the time, Pallas kernels for 38%

commit v1 on v0

v1 whole, which is shorter than its diff:
```python
import functools

import jax
import jax.numpy as jnp
from jax import lax
from jax.experimental import pallas as pl
from jax.experimental.pallas import tpu as pltpu
from jax.sharding import PartitionSpec as P

WIDTH = 256
ROWS = 4
REACH = 4
CELLS = ROWS * WIDTH
OBS = 512
M = 1024
CHUNK = 16
PREP_VMEM = 61 * 1024 * 1024
VMEM = 20 * 1024 * 1024
F32 = jnp.float32
BF16 = jnp.bfloat16


def params():
    return pltpu.CompilerParams(vmem_limit_bytes=VMEM)


def cost(flops, nbytes):
    return pl.CostEstimate(flops=int(flops), bytes_accessed=int(nbytes), transcendentals=0)


def column(row):
    return jnp.broadcast_to(row, (8, row.shape[1])).T[:, 0:1]


def prep_kernel(
    row0_ref, state_ref, pos_ref, side_ref, value_ref, sigma_ref, noise_ref,
    x_ref, p_ref, w_ref, hi_scr, lo_scr, m_scr, noise_scr, sem,
):
    r = pl.program_id(0)
    fetch = pltpu.make_async_copy(noise_ref, noise_scr, sem)

    @pl.when(r == 0)
    def _():
        fetch.start()

    s = state_ref[...]
    ms = jnp.mean(s, axis=1, keepdims=True)
    sd = s - ms
    x_ref[...] = sd.astype(BF16)
    dev = 0.5 * (sd + pltpu.roll(sd, WIDTH - 1, 0))
    hi = dev.astype(BF16)
    here = pl.ds(pl.multiple_of(r * WIDTH, WIDTH), WIDTH)
    hi_scr[here, :] = hi
    lo_scr[here, :] = (dev - hi.astype(F32)).astype(BF16)
    mw = jnp.broadcast_to(ms, (WIDTH, 128))
    pm = 0.5 * (mw + pltpu.roll(mw, WIDTH - 1, 0))
    p0 = pm.astype(BF16).astype(F32)
    p1 = (pm - p0).astype(BF16).astype(F32)
    p2 = pm - p0 - p1
    lane = lax.broadcasted_iota(jnp.int32, (WIDTH, 128), 1)
    m_scr[here, :] = jnp.where(
        lane == 0, p0, jnp.where(lane == 1, p1, jnp.where(lane == 2, p2, 0.0))
    ).astype(BF16)

    @pl.when(r == ROWS - 1)
    def _():
        local = pos_ref[0:1, :] - row0_ref[0]
        col = pos_ref[1:2, :]
        left = (col + side_ref[...] - 1) & (WIDTH - 1)
        sub = lax.broadcasted_iota(jnp.int32, (16, OBS), 0)
        code = jnp.where(sub == 0, local.astype(F32), jnp.where(sub == 1, col.astype(F32), 0.0))
        p_ref[OBS : OBS + 16, 0:OBS] = code.astype(BF16)
        p_ref[OBS : OBS + 16, OBS:M] = jnp.zeros((16, M - OBS), BF16)
        index = column((local * WIDTH + left).astype(F32)).astype(jnp.int32)
        value = column(value_ref[...])
        sigma = column(sigma_ref[...])
        fetch.wait()
        for b in range(4):
            obs = slice(b * 128, (b + 1) * 128)
            cells = lax.broadcasted_iota(jnp.int32, (128, CELLS), 1)
            pick = jnp.where(cells == index[obs], 1.0, 0.0).astype(BF16)
            high = jnp.dot(pick, hi_scr[...], preferred_element_type=F32)
            low = jnp.dot(pick, lo_scr[...], preferred_element_type=F32)
            p_ref[obs, :] = high.astype(BF16)
            dev_o = high + low
            mg = jnp.dot(pick, m_scr[...], preferred_element_type=F32)
            base = value[obs] - jnp.sum(mg, axis=1, keepdims=True)
            spread = jnp.sum(dev_o * dev_o, axis=1, keepdims=True) * (1.0 / (M - 1))
            scale = 1.0 / (spread + sigma[obs] * sigma[obs])
            w = (base + sigma[obs] * noise_scr[obs, :] - dev_o) * scale
            w_ref[obs, :] = w.astype(BF16)


def prep(row0, state, pos, side, value, sigma, noise):
    full = lambda shape: pl.BlockSpec(shape, lambda r: (0,) * len(shape))
    tile = pl.BlockSpec((WIDTH, M), lambda r: (r, 0))
    return pl.pallas_call(
        prep_kernel,
        grid=(ROWS,),
        in_specs=[
            pl.BlockSpec(memory_space=pltpu.SMEM),
            tile,
            full((2, OBS)),
            full((1, OBS)),
            full((1, OBS)),
            full((1, OBS)),
            pl.BlockSpec(memory_space=pl.ANY),
        ],
        out_specs=[tile, full((OBS + 16, M)), full((OBS, M))],
        out_shape=[
            jax.ShapeDtypeStruct((CELLS, M), BF16),
            jax.ShapeDtypeStruct((OBS + 16, M), BF16),
            jax.ShapeDtypeStruct((OBS, M), BF16),
        ],
        scratch_shapes=[
            pltpu.VMEM((CELLS, M), BF16),
            pltpu.VMEM((CELLS, M), BF16),
            pltpu.VMEM((CELLS, 128), BF16),
            pltpu.VMEM((OBS, M), F32),
            pltpu.SemaphoreType.DMA,
        ],
        compiler_params=pltpu.CompilerParams(
            vmem_limit_bytes=PREP_VMEM, dimension_semantics=("arbitrary",)
        ),
        cost_estimate=cost(1 << 20, 1 << 16),
        name="prep",
    )(row0, state, pos, side, value, sigma, noise)


def covariance(x, a_ref, cov_ref):
    cov_ref[...] = lax.dot_general(
        x, a_ref[0:OBS, :], (((1,), (1,)), ((), ())), preferred_element_type=F32
    )


def gain_rows(r, a_ref, offset, cov_ref, g_ref):
    code = a_ref[OBS : OBS + 16, 0:OBS].astype(F32)
    gap = jnp.abs(code[0:1, :] + (ROWS * offset - r).astype(F32))
    row2 = jnp.where(gap > REACH * ROWS, 1e4, jnp.maximum(gap * gap * (1.0 / 256.0), 1e-12))
    col = code[1:2, :] * (1.0 / 16.0)
    n1 = 1.0 / (M - 1)
    for i in range(WIDTH // CHUNK):
        rows = slice(i * CHUNK, (i + 1) * CHUNK)
        q = (lax.broadcasted_iota(jnp.int32, (CHUNK, 1), 0) + i * CHUNK).astype(F32) * (1.0 / 16.0)
        d = jnp.abs(q - col)
        d = jnp.minimum(d, 16.0 - d)
        z2 = d * d + row2
        inv = lax.rsqrt(z2)
        z = z2 * inv
        near = z2 * (z * ((0.625 * n1) + z * ((0.5 * n1) - (0.25 * n1) * z)) - (5.0 / 3.0 * n1)) + n1
        u = jnp.maximum(2.0 - z, 0.0)
        u2 = u * u
        far = (u2 * u2) * ((z2 + (2.0 * z - 0.5)) * (inv * (n1 / 12.0)))
        g_ref[rows, :] = (jnp.where(z2 <= 1.0, near, far) * cov_ref[rows, :]).astype(BF16)


def in_vmem():
    return pl.BlockSpec(memory_space=pltpu.VMEM)


def in_smem():
    return pl.BlockSpec(memory_space=pltpu.SMEM)


def contribute_kernel(distances, sign_ref, x_ref, *refs):
    n = len(distances)
    a_refs = refs[0:n]
    w_refs = refs[n : 2 * n]
    acc_ref, out_ref, cov_scr, g_scr = refs[2 * n :]

    @pl.loop(0, ROWS)
    def _(r):
        here = pl.ds(pl.multiple_of(r * WIDTH, WIDTH), WIDTH)
        for k in range(n):
            covariance(x_ref[here, :], a_refs[k], cov_scr.at[k])
        for k, distance in enumerate(distances):
            gain_rows(r, a_refs[k], sign_ref[0] * distance, cov_scr.at[k], g_scr.at[k])
        for h in range(2):
            part = slice(h * (M // 2), (h + 1) * (M // 2))
            total = acc_ref[here, part]
            for k in range(n):
                total = total + jnp.dot(
                    g_scr[k], w_refs[k][:, part], preferred_element_type=F32
                )
            out_ref[here, part] = total


def contribute(sign, x, packets, distances, acc, first=False):
    n = len(distances)
    return pl.pallas_call(
        functools.partial(contribute_kernel, distances),
        in_specs=[in_smem()] + [in_vmem()] * (2 * n + 2),
        out_specs=in_vmem(),
        out_shape=jax.ShapeDtypeStruct((CELLS, M), F32),
        scratch_shapes=[pltpu.VMEM((n, WIDTH, OBS), F32), pltpu.VMEM((n, WIDTH, OBS), BF16)],
        input_output_aliases={} if first else {2 + 2 * n: 0},
        compiler_params=params(),
        cost_estimate=cost(1 << 20, 1 << 16),
        name="contribute",
    )(sign, x, *[a for a, _ in packets], *[w for _, w in packets], acc)


def gain_kernel(distance, sign_ref, x_ref, a_ref, g_ref, cov_scr):
    @pl.loop(0, ROWS)
    def _(r):
        here = pl.ds(pl.multiple_of(r * WIDTH, WIDTH), WIDTH)
        covariance(x_ref[here, :], a_ref, cov_scr)
        gain_rows(r, a_ref, sign_ref[0] * distance, cov_scr, g_ref.at[here])


def gains(sign, x, a, distance):
    return pl.pallas_call(
        functools.partial(gain_kernel, distance),
        in_specs=[in_smem(), in_vmem(), in_vmem()],
        out_specs=in_vmem(),
        out_shape=jax.ShapeDtypeStruct((CELLS, OBS), BF16),
        scratch_shapes=[pltpu.VMEM((WIDTH, OBS), F32)],
        compiler_params=params(),
        cost_estimate=cost(1 << 20, 1 << 16),
        name="gains",
    )(sign, x, a)


def edge_kernel(sign_ref, acc_ref, g_ref, w_ref, out_ref, cross_ref, inner_ref):
    for i in range(2):
        here = slice(3 * i * WIDTH, (3 * i + 1) * WIDTH)
        for h in range(4):
            part = slice(h * (M // 4), (h + 1) * (M // 4))
            total = acc_ref[here, part] + jnp.dot(
                g_ref[here, :], w_ref[:, part], preferred_element_type=F32
            )
            out_ref[here, part] = total
            outward = 2 * i - 1 == sign_ref[0]

            @pl.when(jnp.logical_not(outward))
            def _():
                inner_ref[:, part] = total.astype(BF16)

            @pl.when(outward)
            def _():
                cross_ref[:, part] = total.astype(BF16)


def edges(sign, acc, gain, w):
    return pl.pallas_call(
        edge_kernel,
        in_specs=[in_smem(), in_vmem(), in_vmem(), in_vmem()],
        out_specs=[in_vmem()] * 3,
        out_shape=[
            jax.ShapeDtypeStruct((CELLS, M), F32),
            jax.ShapeDtypeStruct((WIDTH, M), BF16),
            jax.ShapeDtypeStruct((WIDTH, M), BF16),
        ],
        input_output_aliases={1: 0},
        compiler_params=params(),
        cost_estimate=cost(1 << 20, 1 << 16),
        name="edges",
    )(sign, acc, gain, w)


def advance(a, above, below):
    right = pltpu.roll(a, WIDTH - 1, 0)
    left = pltpu.roll(a, 1, 0)
    pull = 0.05 * a * (above - below + (right - left))
    spread = 0.2 * (above + below + right + left - 4.0 * a)
    return a - pull + spread


def middle_kernel(acc_ref, g_ref, w_ref, mid_ref, out_ref, pred_scr, sems):
    rows = lambda r: slice(r * WIDTH, (r + 1) * WIDTH)
    copies = []
    for h in range(4):
        part = slice(h * (M // 4), (h + 1) * (M // 4))
        mids = []
        for i in range(2):
            total = acc_ref[rows(1 + i), part] + jnp.dot(
                g_ref[rows(1 + i), :], w_ref[:, part], preferred_element_type=F32
            )
            mid_ref[rows(i), part] = total
            mids.append(total)
        pred_scr[rows(0), part] = advance(mids[0], mids[1], acc_ref[rows(0), part])
        pred_scr[rows(1), part] = advance(mids[1], acc_ref[rows(3), part], mids[0])
        copies.append(
            pltpu.make_async_copy(
                pred_scr.at[:, part], out_ref.at[WIDTH : 3 * WIDTH, part], sems.at[h]
            )
        )
        copies[-1].start()
    for copy in copies:
        copy.wait()


def middle(acc, gain, w):
    return pl.pallas_call(
        middle_kernel,
        in_specs=[in_vmem()] * 3,
        out_specs=[in_vmem(), pl.BlockSpec(memory_space=pl.ANY)],
        out_shape=[
            jax.ShapeDtypeStruct((2 * WIDTH, M), F32),
            jax.ShapeDtypeStruct((CELLS, M), F32),
        ],
        scratch_shapes=[pltpu.VMEM((2 * WIDTH, M), F32), pltpu.SemaphoreType.DMA((4,))],
        compiler_params=params(),
        cost_estimate=cost(1 << 20, 1 << 16),
        name="middle",
    )(acc, gain, w)


def outer_kernel(sign_ref, acc_ref, mid_ref, cross_ref, inner_ref, _, out_ref, pred_scr, sems):
    rows = lambda r: slice(r * WIDTH, (r + 1) * WIDTH)
    first = sign_ref[0] < 0
    copies = []
    for h in range(4):
        part = slice(h * (M // 4), (h + 1) * (M // 4))
        cross = cross_ref[:, part].astype(F32)
        inner = inner_ref[:, part].astype(F32)
        before = jnp.where(first, cross, inner)
        after = jnp.where(first, inner, cross)
        pred_scr[rows(0), part] = advance(acc_ref[rows(0), part], mid_ref[rows(0), part], before)
        pred_scr[rows(1), part] = advance(acc_ref[rows(3), part], after, mid_ref[rows(1), part])
        for i in range(2):
            copies.append(
                pltpu.make_async_copy(
                    pred_scr.at[rows(i), part], out_ref.at[rows(3 * i), part], sems.at[2 * h + i]
                )
            )
            copies[-1].start()
    for copy in copies:
        copy.wait()


def outer(sign, acc, mid, cross, inner, out):
    return pl.pallas_call(
        outer_kernel,
        in_specs=[in_smem()] + [in_vmem()] * 4 + [pl.BlockSpec(memory_space=pl.ANY)],
        out_specs=pl.BlockSpec(memory_space=pl.ANY),
        out_shape=jax.ShapeDtypeStruct((CELLS, M), F32),
        scratch_shapes=[pltpu.VMEM((2 * WIDTH, M), F32), pltpu.SemaphoreType.DMA((8,))],
        input_output_aliases={5: 0},
        compiler_params=params(),
        cost_estimate=cost(1 << 20, 1 << 16),
        name="outer",
    )(sign, acc, mid, cross, inner, out)


def hold(value, acc):
    held, acc = lax.optimization_barrier((value, acc))
    return held, acc


def on_device(state, obs_value, obs_sigma, obs_noise, obs_pos, obs_side):
    device = lax.axis_index("space")
    slabs = lax.axis_size("space")
    pairs = [(i, i ^ 1) for i in range(slabs)]
    across = [(i, (i + 1 if i % 2 else i - 1) % slabs) for i in range(slabs)]
    inside = lambda block: lax.ppermute(block, "space", pairs)
    beyond = lambda block: lax.ppermute(block, "space", across)
    row0 = (device * ROWS).astype(jnp.int32).reshape(1)
    sign = (2 * (device % 2) - 1).astype(jnp.int32).reshape(1)
    row = lambda v: v.reshape(1, OBS)
    x, own_a, own_w = prep(
        row0, state, obs_pos, row(obs_side), row(obs_value), row(obs_sigma), obs_noise
    )

    one_a, one_w = beyond(own_a), beyond(own_w)
    twin_a, twin_w = inside(own_a), inside(own_w)
    two_a, two_w = beyond(twin_a), beyond(twin_w)
    acc = contribute(sign, x, ((own_a, own_w), (twin_a, twin_w)), (0, -1), state, True)
    one_a, acc = hold(one_a, acc)
    one_twin_a, one_twin_w = inside(one_a), inside(one_w)
    three_a, three_w = beyond(one_twin_a), beyond(one_twin_w)
    acc = contribute(sign, x, ((one_a, one_w), (one_twin_a, one_twin_w)), (1, -2), acc)
    two_a, acc = hold(two_a, acc)
    two_twin_a, two_twin_w = inside(two_a), inside(two_w)
    four_a, four_w = beyond(two_twin_a), beyond(two_twin_w)
    acc = contribute(sign, x, ((two_a, two_w), (two_twin_a, two_twin_w)), (2, -3), acc)
    three_a, acc = hold(three_a, acc)
    three_twin_a, three_twin_w = inside(three_a), inside(three_w)
    acc = contribute(sign, x, ((three_a, three_w), (three_twin_a, three_twin_w)), (3, -4), acc)
    four_a, acc = hold(four_a, acc)
    gain = gains(sign, x, four_a, 4)
    acc, to_cross, to_inner = edges(sign, acc, gain, four_w)
    cross, inner = beyond(to_cross), inside(to_inner)
    mid, out = middle(acc, gain, four_w)
    return outer(sign, acc, mid, cross, inner, out)


def solution(mesh):
    placed = (
        P("space", None),
        P("space"),
        P("space"),
        P("space", None),
        P(None, "space"),
        P("space"),
    )
    return jax.shard_map(
        on_device, mesh=mesh, in_specs=placed, out_specs=P("space", None), check_vma=False
    )
```

time: 153 us -> 133 us (0.87)
  Pallas kernels: 72.7 us -> 55.3 us
  starting transfers between devices: 56.4 us -> 41.4 us
  waiting for transfers between devices: 19 us -> 29.7 us
  local copies, waits for them, and re-layouts: 4.09 us -> 6.25 us
    pallas_call x9 -> x8, Pallas kernels: 65.4 us -> 45.8 us  [the longest x4 35 us: contribute(): pl.pallas_call(functools.partial(contribute_kernel, distances), in_specs=...]
    ppermute x18, starting transfers between devices: 56.4 us -> 41.4 us  [the longest x9 41 us: on_device(): beyond = lambda block: lax.ppermute(block, 'space', across)]
    ppermute x18, waiting for transfers between devices: 19 us -> 29.7 us  [the longest x9 27.3 us: on_device(): beyond = lambda block: lax.ppermute(block, 'space', across)]
    unnamed x18 -> x10, local copies, waits for them, and re-layouts: 4.02 us -> 6.25 us
    pallas_call x1, Pallas kernels: 7.31 us -> 9.49 us  [prep(): pl.pallas_call(prep_kernel, grid=(ROWS,), in_specs=[pl.BlockSpec(memory_s...]
  transfers between devices with their start and end apart: 18 -> 18, of which waited for: 3 -> 6; matrix products, arithmetic and copies ran while one was open for 0% -> 0% of each run, Pallas kernels for 38% -> 31%
where the time goes in v1:
time: 133 us
  Pallas kernels  55.3 us (42%)
  starting transfers between devices  41.4 us (31%)
  waiting for transfers between devices  29.7 us (22%)
  local copies, waits for them, and re-layouts  6.25 us (5%)
    ppermute x9, starting transfers between devices, on_device(): beyond = lambda block: lax.ppermute(block, 'space', across)  41 us
    pallas_call x4, Pallas kernels, contribute(): pl.pallas_call(functools.partial(contribute_kernel, distances), in_specs=...  35 us
    ppermute x9, waiting for transfers between devices, on_device(): beyond = lambda block: lax.ppermute(block, 'space', across)  27.3 us
    pallas_call x1, Pallas kernels, prep(): pl.pallas_call(prep_kernel, grid=(ROWS,), in_specs=[pl.BlockSpec(memory_s...  9.49 us
    unnamed x10, local copies, waits for them, and re-layouts  6.25 us
    pallas_call x1, Pallas kernels, gains(): pl.pallas_call(functools.partial(gain_kernel, distance), in_specs=[in_sme...  3.38 us
  transfers between devices with their start and end apart: 18, of which 6 were waited for; matrix products, arithmetic and copies ran while one was open for 0% of the time, Pallas kernels for 31%

profile of v1, /device:TPU:0, one launch (start us, length us, event | category | flops | bytes accessed | tf_op | source)
XLA Modules:
  0.0 133.0 jit_solution(4315920451282771954)
XLA Ops:
  0.0 9.5 %prep.1 = (bf16[1024,1024]{1,0:T(8,128)(2,1)}, bf16[528,1024]{1,0:T(8,128)(2,1)}, bf16[512,1024]{1,0:T(8,128)(2,1)}) custom-call(s32[1]{0:T(128)} %bitcast.1.row0_ref, f32[1024,1024]{1,0:T(8,128)} %refs_4_.1, s32[2,512]{1,0:T(2,128)} %pos_ref.1, s32[1,512]{1,0:T(1,128)} %bitcast.5, f32[1,512]{1,0:T(1,128)} %bitcast.6, f32[1,512]{1,0:T(1,128)} %bitcast.7, ...), custom_call_target="tpu_custom_call" | custom-call | flops 1048576 | bytes 65536 | tf_op jit(solution)/shard_map/prep/pallas_call | solution.py:97
  9.5 0.1 collective-permute-start
  9.6 8.9 %collective-permute-start.2 = (bf16[528,1024]{1,0:T(8,128)(2,1)}, bf16[528,1024]{1,0:T(8,128)(2,1)S(1)}, u32[]{:S(2)}, u32[]{:S(2)}) collective-permute-start(bf16[528,1024]{1,0:T(8,128)(2,1)} %get-tuple-element.21.refs_0_), channel_id=1, source_target_pairs={{0,127},{1,2},{2,1},{3,4},{4,3},{5,6},{6,5},{7,8},{8,7},{9,10},{10... | collective-permute-start | bytes 3244040 | tf_op jit(solution)/shard_map/ppermute | solution.py:357
  18.5 0.5 collective-permute-start.5
  19.0 2.4 %collective-permute-done.3.refs_3_ = bf16[512,1024]{1,0:T(8,128)(2,1)S(1)} collective-permute-done((bf16[512,1024]{1,0:T(8,128)(2,1)}, bf16[512,1024]{1,0:T(8,128)(2,1)S(1)}, u32[]{:S(2)}, u32[]{:S(2)}) %collective-permute-start.3) | collective-permute-done | bytes 1048608 | tf_op jit(solution)/shard_map/ppermute | solution.py:356
  21.3 1.6 %copy-done = bf16[1024,1024]{1,0:T(8,128)(2,1)S(1)} copy-done((bf16[1024,1024]{1,0:T(8,128)(2,1)S(1)}, bf16[1024,1024]{1,0:T(8,128)(2,1)}, u32[]{:S(2)}) %copy-start) | copy-done | bytes 2097176
  22.9 2.2 %copy-done.2 = f32[1024,1024]{1,0:T(8,128)S(1)} copy-done((f32[1024,1024]{1,0:T(8,128)S(1)}, f32[1024,1024]{1,0:T(8,128)}, u32[]{:S(2)}) %copy-start.2) | copy-done | bytes 4194328
  25.1 1.2 copy-done.3
  26.4 1.2 copy-done.4
  27.6 8.4 %contribute.4.refs_4_ = f32[1024,1024]{1,0:T(8,128)S(1)} custom-call(s32[1]{0:T(128)} %bitcast.sign_ref, bf16[1024,1024]{1,0:T(8,128)(2,1)S(1)} %copy-done, bf16[528,1024]{1,0:T(8,128)(2,1)S(1)} %copy-done.3, bf16[528,1024]{1,0:T(8,128)(2,1)S(1)} %collective-permute-done.refs_1_, bf16[512,1024]{1,0:T(8,128)(2,1)S(1)} %copy-done.4, ...), custom_call_target="tpu_custom_call" | custom-call | flops 1048576 | bytes 65536 | tf_op jit(solution)/shard_map/contribute/pallas_call | solution.py:190
  36.0 0.2 collective-permute-start.4
  36.2 4.3 %collective-permute-start.1 = (bf16[528,1024]{1,0:T(8,128)(2,1)S(1)}, bf16[528,1024]{1,0:T(8,128)(2,1)S(1)}, u32[]{:S(2)}, u32[]{:S(2)}) collective-permute-start(bf16[528,1024]{1,0:T(8,128)(2,1)S(1)} %collective-permute-done.refs_1_), channel_id=1, source_target_pairs={{0,127},{1,2},{2,1},{3,4},{4,3},{5,6},{6,5},{7,8},{8,7},{9,10},{10... | collective-permute-start | bytes 3244040 | tf_op jit(solution)/shard_map/ppermute | solution.py:357
  40.5 2.3 %collective-permute-done.5.refs_2_ = bf16[512,1024]{1,0:T(8,128)(2,1)} collective-permute-done((bf16[512,1024]{1,0:T(8,128)(2,1)}, bf16[512,1024]{1,0:T(8,128)(2,1)}, u32[]{:S(2)}, u32[]{:S(2)}) %collective-permute-start.5) | collective-permute-done | bytes 1048608 | tf_op jit(solution)/shard_map/ppermute | solution.py:357
  42.8 7.2 %collective-permute-start.10 = (bf16[512,1024]{1,0:T(8,128)(2,1)S(1)}, bf16[512,1024]{1,0:T(8,128)(2,1)S(1)}, u32[]{:S(2)}, u32[]{:S(2)}) collective-permute-start(bf16[512,1024]{1,0:T(8,128)(2,1)S(1)} %collective-permute-done.3.refs_3_), channel_id=1, source_target_pairs={{0,127},{1,2},{2,1},{3,4},{4,3},{5,6},{6,5},{7,8},{8,7},{9,10},{10... | collective-permute-start | bytes 3145736 | tf_op jit(solution)/shard_map/ppermute | solution.py:357
  50.0 9.7 %contribute.5.refs_4_ = f32[1024,1024]{1,0:T(8,128)S(1)} custom-call(s32[1]{0:T(128)} %bitcast.sign_ref, bf16[1024,1024]{1,0:T(8,128)(2,1)S(1)} %copy-done, bf16[528,1024]{1,0:T(8,128)(2,1)S(1)} %collective-permute-done.2.refs_0_, bf16[528,1024]{1,0:T(8,128)(2,1)S(1)} %collective-permute-done.4.refs_1_, ...), custom_call_target="tpu_custom_call", output_to_operand_aliasing={{}: (6, {})} | custom-call | flops 1048576 | bytes 65536 | tf_op jit(solution)/shard_map/contribute/pallas_call | solution.py:190
  59.7 0.1 collective-permute-start.7
  59.8 3.0 %collective-permute-start.9 = (bf16[528,1024]{1,0:T(8,128)(2,1)S(1)}, bf16[528,1024]{1,0:T(8,128)(2,1)S(1)}, u32[]{:S(2)}, u32[]{:S(2)}) collective-permute-start(bf16[528,1024]{1,0:T(8,128)(2,1)S(1)} %collective-permute-done.4.refs_1_), channel_id=1, source_target_pairs={{0,127},{1,2},{2,1},{3,4},{4,3},{5,6},{6,5},{7,8},{8,7},{9,10},{10... | collective-permute-start | bytes 3244040 | tf_op jit(solution)/shard_map/ppermute | solution.py:357
  62.8 4.7 %collective-permute-done.10.refs_2_ = bf16[512,1024]{1,0:T(8,128)(2,1)S(1)} collective-permute-done((bf16[512,1024]{1,0:T(8,128)(2,1)S(1)}, bf16[512,1024]{1,0:T(8,128)(2,1)S(1)}, u32[]{:S(2)}, u32[]{:S(2)}) %collective-permute-start.10) | collective-permute-done | bytes 1048608 | tf_op jit(solution)/shard_map/ppermute | solution.py:357
  67.5 5.3 %collective-permute-start.13 = (bf16[512,1024]{1,0:T(8,128)(2,1)S(1)}, bf16[512,1024]{1,0:T(8,128)(2,1)S(1)}, u32[]{:S(2)}, u32[]{:S(2)}) collective-permute-start(bf16[512,1024]{1,0:T(8,128)(2,1)S(1)} %collective-permute-done.6.refs_3_), channel_id=1, source_target_pairs={{0,127},{1,2},{2,1},{3,4},{4,3},{5,6},{6,5},{7,8},{8,7},{9,10},{10... | collective-permute-start | bytes 3145736 | tf_op jit(solution)/shard_map/ppermute | solution.py:357
  72.7 8.5 %contribute.6.refs_4_ = f32[1024,1024]{1,0:T(8,128)S(1)} custom-call(s32[1]{0:T(128)} %bitcast.sign_ref, bf16[1024,1024]{1,0:T(8,128)(2,1)S(1)} %copy-done, bf16[528,1024]{1,0:T(8,128)(2,1)S(1)} %collective-permute-done.1.refs_0_, bf16[528,1024]{1,0:T(8,128)(2,1)S(1)} %collective-permute-done.7.refs_1_, ...), custom_call_target="tpu_custom_call", output_to_operand_aliasing={{}: (6, {})} | custom-call | flops 1048576 | bytes 65536 | tf_op jit(solution)/shard_map/contribute/pallas_call | solution.py:190
  81.2 0.1 collective-permute-start.12
  81.3 3.0 %collective-permute-start.8 = (bf16[528,1024]{1,0:T(8,128)(2,1)S(1)}, bf16[528,1024]{1,0:T(8,128)(2,1)S(1)}, u32[]{:S(2)}, u32[]{:S(2)}) collective-permute-start(bf16[528,1024]{1,0:T(8,128)(2,1)S(1)} %collective-permute-done.7.refs_1_), channel_id=1, source_target_pairs={{0,127},{1,2},{2,1},{3,4},{4,3},{5,6},{6,5},{7,8},{8,7},{9,10},{10... | collective-permute-start | bytes 3244040 | tf_op jit(solution)/shard_map/ppermute | solution.py:357
  84.3 6.8 %collective-permute-done.13.refs_2_ = bf16[512,1024]{1,0:T(8,128)(2,1)S(1)} collective-permute-done((bf16[512,1024]{1,0:T(8,128)(2,1)S(1)}, bf16[512,1024]{1,0:T(8,128)(2,1)S(1)}, u32[]{:S(2)}, u32[]{:S(2)}) %collective-permute-start.13) | collective-permute-done | bytes 1048608 | tf_op jit(solution)/shard_map/ppermute | solution.py:357
  91.2 4.4 %collective-permute-start.15 = (bf16[512,1024]{1,0:T(8,128)(2,1)S(1)}, bf16[512,1024]{1,0:T(8,128)(2,1)S(1)}, u32[]{:S(2)}, u32[]{:S(2)}) collective-permute-start(bf16[512,1024]{1,0:T(8,128)(2,1)S(1)} %collective-permute-done.11.refs_3_), channel_id=1, source_target_pairs={{0,127},{1,2},{2,1},{3,4},{4,3},{5,6},{6,5},{7,8},{8,7},{9,10},{10... | collective-permute-start | bytes 3145736 | tf_op jit(solution)/shard_map/ppermute | solution.py:357
  95.6 8.5 %contribute.7.acc_ref = f32[1024,1024]{1,0:T(8,128)S(1)} custom-call(s32[1]{0:T(128)} %bitcast.sign_ref, bf16[1024,1024]{1,0:T(8,128)(2,1)S(1)} %copy-done, bf16[528,1024]{1,0:T(8,128)(2,1)S(1)} %collective-permute-done.9.refs_0_, bf16[528,1024]{1,0:T(8,128)(2,1)S(1)} %collective-permute-done.12.refs_1_, ...), custom_call_target="tpu_custom_call", output_to_operand_aliasing={{}: (6, {})} | custom-call | flops 1048576 | bytes 65536 | tf_op jit(solution)/shard_map/contribute/pallas_call | solution.py:190
  104.1 3.4 %gains.1.g_ref = bf16[1024,512]{1,0:T(8,128)(2,1)S(1)} custom-call(s32[1]{0:T(128)} %bitcast.sign_ref, bf16[1024,1024]{1,0:T(8,128)(2,1)S(1)} %copy-done.1, bf16[528,1024]{1,0:T(8,128)(2,1)S(1)} %collective-permute-done.8.a_ref), custom_call_target="tpu_custom_call" | custom-call | flops 1048576 | bytes 65536 | tf_op jit(solution)/shard_map/gains/pallas_call | solution.py:212
  107.4 6.5 %collective-permute-done.15.w_ref = bf16[512,1024]{1,0:T(8,128)(2,1)S(1)} collective-permute-done((bf16[512,1024]{1,0:T(8,128)(2,1)S(1)}, bf16[512,1024]{1,0:T(8,128)(2,1)S(1)}, u32[]{:S(2)}, u32[]{:S(2)}) %collective-permute-start.15) | collective-permute-done | bytes 1048608 | tf_op jit(solution)/shard_map/ppermute | solution.py:357
  114.0 2.5 %edges.1 = (f32[1024,1024]{1,0:T(8,128)S(1)}, bf16[256,1024]{1,0:T(8,128)(2,1)S(1)}, bf16[256,1024]{1,0:T(8,128)(2,1)S(1)}) custom-call(s32[1]{0:T(128)} %bitcast.sign_ref, f32[1024,1024]{1,0:T(8,128)S(1)} %contribute.7.acc_ref, bf16[1024,512]{1,0:T(8,128)(2,1)S(1)} %gains.1.g_ref, ...), custom_call_target="tpu_custom_call", output_to_operand_aliasing={{0}: (1, {})} | custom-call | flops 1048576 | bytes 65536 | tf_op jit(solution)/shard_map/edges/pallas_call | solution.py:245
  116.5 4.5 %collective-permute-start.16 = (bf16[256,1024]{1,0:T(8,128)(2,1)S(1)}, bf16[256,1024]{1,0:T(8,128)(2,1)S(1)}, u32[]{:S(2)}, u32[]{:S(2)}) collective-permute-start(bf16[256,1024]{1,0:T(8,128)(2,1)S(1)} %get-tuple-element.34), channel_id=1, source_target_pairs={{0,127},{1,2},{2,1},{3,4},{4,3},{5,6},{6,5},{7,8},{8,7},{9,10},{10... | collective-permute-start | bytes 1572872 | tf_op jit(solution)/shard_map/ppermute | solution.py:357
  120.9 2.6 %middle.1 = (f32[512,1024]{1,0:T(8,128)S(1)}, f32[1024,1024]{1,0:T(8,128)}) custom-call(f32[1024,1024]{1,0:T(8,128)S(1)} %get-tuple-element.32.acc_ref, bf16[1024,512]{1,0:T(8,128)(2,1)S(1)} %gains.1.g_ref, bf16[512,1024]{1,0:T(8,128)(2,1)S(1)} %collective-permute-done.15.w_ref), custom_call_target="tpu_custom_call" | custom-call | flops 1048576 | bytes 65536 | tf_op jit(solution)/shard_map/middle/pallas_call | solution.py:294
  123.6 7.0 %collective-permute-done.16.cross_ref = bf16[256,1024]{1,0:T(8,128)(2,1)S(1)} collective-permute-done((bf16[256,1024]{1,0:T(8,128)(2,1)S(1)}, bf16[256,1024]{1,0:T(8,128)(2,1)S(1)}, u32[]{:S(2)}, u32[]{:S(2)}) %collective-permute-start.16) | collective-permute-done | bytes 524320 | tf_op jit(solution)/shard_map/ppermute | solution.py:357
  130.6 2.3 %outer.1 = f32[1024,1024]{1,0:T(8,128)} custom-call(s32[1]{0:T(128)} %bitcast.sign_ref, f32[1024,1024]{1,0:T(8,128)S(1)} %get-tuple-element.32.acc_ref, f32[512,1024]{1,0:T(8,128)S(1)} %get-tuple-element.33.mid_ref, bf16[256,1024]{1,0:T(8,128)(2,1)S(1)} %collective-permute-done.16.cross_ref, ...), custom_call_target="tpu_custom_call", output_to_operand_aliasing={{}: (5, {})} | custom-call | flops 1048576 | bytes 65536 | tf_op jit(solution)/shard_map/outer/pallas_call | solution.py:333
  (23 shorter events, 0.1 us)
Async XLA Ops:
  9.5 11.8 %collective-permute-start = (bf16[528,1024]{1,0:T(8,128)(2,1)}, bf16[528,1024]{1,0:T(8,128)(2,1)S(1)}, u32[]{:S(2)}, u32[]{:S(2)}) collective-permute-start(bf16[528,1024]{1,0:T(8,128)(2,1)} %get-tuple-element.21.refs_0_), channel_id=1, source_target_pairs={{0,1},{1,0},{2,3},{3,2},{4,5},{5,4},{6,7},{7,6},{8,9},{9,8},{10,11... | collective-permute-start | bytes 3244040 | tf_op jit(solution)/shard_map/ppermute | solution.py:356
  9.6 26.4 %collective-permute-start.2 = (bf16[528,1024]{1,0:T(8,128)(2,1)}, bf16[528,1024]{1,0:T(8,128)(2,1)S(1)}, u32[]{:S(2)}, u32[]{:S(2)}) collective-permute-start(bf16[528,1024]{1,0:T(8,128)(2,1)} %get-tuple-element.21.refs_0_), channel_id=1, source_target_pairs={{0,127},{1,2},{2,1},{3,4},{4,3},{5,6},{6,5},{7,8},{8,7},{9,10},{10... | collective-permute-start | bytes 3244040 | tf_op jit(solution)/shard_map/ppermute | solution.py:357
  18.5 2.9 %collective-permute-start.3 = (bf16[512,1024]{1,0:T(8,128)(2,1)}, bf16[512,1024]{1,0:T(8,128)(2,1)S(1)}, u32[]{:S(2)}, u32[]{:S(2)}) collective-permute-start(bf16[512,1024]{1,0:T(8,128)(2,1)} %get-tuple-element.23.refs_2_), channel_id=1, source_target_pairs={{0,1},{1,0},{2,3},{3,2},{4,5},{5,4},{6,7},{7,6},{8,9},{9,8},{10,11... | collective-permute-start | bytes 3145736 | tf_op jit(solution)/shard_map/ppermute | solution.py:356
  18.5 24.4 %collective-permute-start.5 = (bf16[512,1024]{1,0:T(8,128)(2,1)}, bf16[512,1024]{1,0:T(8,128)(2,1)}, u32[]{:S(2)}, u32[]{:S(2)}) collective-permute-start(bf16[512,1024]{1,0:T(8,128)(2,1)} %get-tuple-element.23.refs_2_), channel_id=1, source_target_pairs={{0,127},{1,2},{2,1},{3,4},{4,3},{5,6},{6,5},{7,8},{8,7},{9,10},{10... | collective-permute-start | bytes 3145736 | tf_op jit(solution)/shard_map/ppermute | solution.py:357
  21.3 1.6 %copy-start = (bf16[1024,1024]{1,0:T(8,128)(2,1)S(1)}, bf16[1024,1024]{1,0:T(8,128)(2,1)}, u32[]{:S(2)}) copy-start(bf16[1024,1024]{1,0:T(8,128)(2,1)} %get-tuple-element.22.x_ref) | copy-start | bytes 6291460
  22.9 2.2 %copy-start.2 = (f32[1024,1024]{1,0:T(8,128)S(1)}, f32[1024,1024]{1,0:T(8,128)}, u32[]{:S(2)}) copy-start(f32[1024,1024]{1,0:T(8,128)} %refs_4_.1) | copy-start | bytes 12582916
  25.1 1.2 copy-start.3
  26.4 1.2 copy-start.4
  36.0 14.0 %collective-permute-start.4 = (bf16[528,1024]{1,0:T(8,128)(2,1)S(1)}, bf16[528,1024]{1,0:T(8,128)(2,1)S(1)}, u32[]{:S(2)}, u32[]{:S(2)}) collective-permute-start(bf16[528,1024]{1,0:T(8,128)(2,1)S(1)} %collective-permute-done.2.refs_0_), channel_id=1, source_target_pairs={{0,1},{1,0},{2,3},{3,2},{4,5},{5,4},{6,7},{7,6},{8,9},{9,8},{10,11... | collective-permute-start | bytes 3244040 | tf_op jit(solution)/shard_map/ppermute | solution.py:356
  36.2 23.5 %collective-permute-start.1 = (bf16[528,1024]{1,0:T(8,128)(2,1)S(1)}, bf16[528,1024]{1,0:T(8,128)(2,1)S(1)}, u32[]{:S(2)}, u32[]{:S(2)}) collective-permute-start(bf16[528,1024]{1,0:T(8,128)(2,1)S(1)} %collective-permute-done.refs_1_), channel_id=1, source_target_pairs={{0,127},{1,2},{2,1},{3,4},{4,3},{5,6},{6,5},{7,8},{8,7},{9,10},{10... | collective-permute-start | bytes 3244040 | tf_op jit(solution)/shard_map/ppermute | solution.py:357
  42.8 7.2 %collective-permute-start.6 = (bf16[512,1024]{1,0:T(8,128)(2,1)}, bf16[512,1024]{1,0:T(8,128)(2,1)S(1)}, u32[]{:S(2)}, u32[]{:S(2)}) collective-permute-start(bf16[512,1024]{1,0:T(8,128)(2,1)} %collective-permute-done.5.refs_2_), channel_id=1, source_target_pairs={{0,1},{1,0},{2,3},{3,2},{4,5},{5,4},{6,7},{7,6},{8,9},{9,8},{10,11... | collective-permute-start | bytes 3145736 | tf_op jit(solution)/shard_map/ppermute | solution.py:356
  42.8 24.6 %collective-permute-start.10 = (bf16[512,1024]{1,0:T(8,128)(2,1)S(1)}, bf16[512,1024]{1,0:T(8,128)(2,1)S(1)}, u32[]{:S(2)}, u32[]{:S(2)}) collective-permute-start(bf16[512,1024]{1,0:T(8,128)(2,1)S(1)} %collective-permute-done.3.refs_3_), channel_id=1, source_target_pairs={{0,127},{1,2},{2,1},{3,4},{4,3},{5,6},{6,5},{7,8},{8,7},{9,10},{10... | collective-permute-start | bytes 3145736 | tf_op jit(solution)/shard_map/ppermute | solution.py:357
  59.7 13.0 %collective-permute-start.7 = (bf16[528,1024]{1,0:T(8,128)(2,1)S(1)}, bf16[528,1024]{1,0:T(8,128)(2,1)S(1)}, u32[]{:S(2)}, u32[]{:S(2)}) collective-permute-start(bf16[528,1024]{1,0:T(8,128)(2,1)S(1)} %collective-permute-done.1.refs_0_), channel_id=1, source_target_pairs={{0,1},{1,0},{2,3},{3,2},{4,5},{5,4},{6,7},{7,6},{8,9},{9,8},{10,11... | collective-permute-start | bytes 3244040 | tf_op jit(solution)/shard_map/ppermute | solution.py:356
  59.8 21.4 %collective-permute-start.9 = (bf16[528,1024]{1,0:T(8,128)(2,1)S(1)}, bf16[528,1024]{1,0:T(8,128)(2,1)S(1)}, u32[]{:S(2)}, u32[]{:S(2)}) collective-permute-start(bf16[528,1024]{1,0:T(8,128)(2,1)S(1)} %collective-permute-done.4.refs_1_), channel_id=1, source_target_pairs={{0,127},{1,2},{2,1},{3,4},{4,3},{5,6},{6,5},{7,8},{8,7},{9,10},{10... | collective-permute-start | bytes 3244040 | tf_op jit(solution)/shard_map/ppermute | solution.py:357
  67.5 5.3 %collective-permute-start.11 = (bf16[512,1024]{1,0:T(8,128)(2,1)S(1)}, bf16[512,1024]{1,0:T(8,128)(2,1)S(1)}, u32[]{:S(2)}, u32[]{:S(2)}) collective-permute-start(bf16[512,1024]{1,0:T(8,128)(2,1)S(1)} %collective-permute-done.10.refs_2_), channel_id=1, source_target_pairs={{0,1},{1,0},{2,3},{3,2},{4,5},{5,4},{6,7},{7,6},{8,9},{9,8},{10,11... | collective-permute-start | bytes 3145736 | tf_op jit(solution)/shard_map/ppermute | solution.py:356
  67.5 23.7 %collective-permute-start.13 = (bf16[512,1024]{1,0:T(8,128)(2,1)S(1)}, bf16[512,1024]{1,0:T(8,128)(2,1)S(1)}, u32[]{:S(2)}, u32[]{:S(2)}) collective-permute-start(bf16[512,1024]{1,0:T(8,128)(2,1)S(1)} %collective-permute-done.6.refs_3_), channel_id=1, source_target_pairs={{0,127},{1,2},{2,1},{3,4},{4,3},{5,6},{6,5},{7,8},{8,7},{9,10},{10... | collective-permute-start | bytes 3145736 | tf_op jit(solution)/shard_map/ppermute | solution.py:357
  81.2 22.8 %copy-start.1 = (bf16[1024,1024]{1,0:T(8,128)(2,1)S(1)}, bf16[1024,1024]{1,0:T(8,128)(2,1)}, u32[]{:S(2)}) copy-start(bf16[1024,1024]{1,0:T(8,128)(2,1)} %get-tuple-element.22.x_ref) | copy-start | bytes 6291460
  81.2 14.3 %collective-permute-start.12 = (bf16[528,1024]{1,0:T(8,128)(2,1)S(1)}, bf16[528,1024]{1,0:T(8,128)(2,1)S(1)}, u32[]{:S(2)}, u32[]{:S(2)}) collective-permute-start(bf16[528,1024]{1,0:T(8,128)(2,1)S(1)} %collective-permute-done.9.refs_0_), channel_id=1, source_target_pairs={{0,1},{1,0},{2,3},{3,2},{4,5},{5,4},{6,7},{7,6},{8,9},{9,8},{10,11... | collective-permute-start | bytes 3244040 | tf_op jit(solution)/shard_map/ppermute | solution.py:356
  81.3 22.7 %collective-permute-start.8 = (bf16[528,1024]{1,0:T(8,128)(2,1)S(1)}, bf16[528,1024]{1,0:T(8,128)(2,1)S(1)}, u32[]{:S(2)}, u32[]{:S(2)}) collective-permute-start(bf16[528,1024]{1,0:T(8,128)(2,1)S(1)} %collective-permute-done.7.refs_1_), channel_id=1, source_target_pairs={{0,127},{1,2},{2,1},{3,4},{4,3},{5,6},{6,5},{7,8},{8,7},{9,10},{10... | collective-permute-start | bytes 3244040 | tf_op jit(solution)/shard_map/ppermute | solution.py:357
  91.1 4.4 %collective-permute-start.14 = (bf16[512,1024]{1,0:T(8,128)(2,1)S(1)}, bf16[512,1024]{1,0:T(8,128)(2,1)S(1)}, u32[]{:S(2)}, u32[]{:S(2)}) collective-permute-start(bf16[512,1024]{1,0:T(8,128)(2,1)S(1)} %collective-permute-done.13.refs_2_), channel_id=1, source_target_pairs={{0,1},{1,0},{2,3},{3,2},{4,5},{5,4},{6,7},{7,6},{8,9},{9,8},{10,11... | collective-permute-start | bytes 3145736 | tf_op jit(solution)/shard_map/ppermute | solution.py:356
  91.2 22.8 %collective-permute-start.15 = (bf16[512,1024]{1,0:T(8,128)(2,1)S(1)}, bf16[512,1024]{1,0:T(8,128)(2,1)S(1)}, u32[]{:S(2)}, u32[]{:S(2)}) collective-permute-start(bf16[512,1024]{1,0:T(8,128)(2,1)S(1)} %collective-permute-done.11.refs_3_), channel_id=1, source_target_pairs={{0,127},{1,2},{2,1},{3,4},{4,3},{5,6},{6,5},{7,8},{8,7},{9,10},{10... | collective-permute-start | bytes 3145736 | tf_op jit(solution)/shard_map/ppermute | solution.py:357
  116.5 14.1 %collective-permute-start.16 = (bf16[256,1024]{1,0:T(8,128)(2,1)S(1)}, bf16[256,1024]{1,0:T(8,128)(2,1)S(1)}, u32[]{:S(2)}, u32[]{:S(2)}) collective-permute-start(bf16[256,1024]{1,0:T(8,128)(2,1)S(1)} %get-tuple-element.34), channel_id=1, source_target_pairs={{0,127},{1,2},{2,1},{3,4},{4,3},{5,6},{6,5},{7,8},{8,7},{9,10},{10... | collective-permute-start | bytes 1572872 | tf_op jit(solution)/shard_map/ppermute | solution.py:357
  120.9 9.6 %collective-permute-start.17 = (bf16[256,1024]{1,0:T(8,128)(2,1)S(1)}, bf16[256,1024]{1,0:T(8,128)(2,1)S(1)}, u32[]{:S(2)}, u32[]{:S(2)}) collective-permute-start(bf16[256,1024]{1,0:T(8,128)(2,1)S(1)} %get-tuple-element.35), channel_id=1, source_target_pairs={{0,1},{1,0},{2,3},{3,2},{4,5},{5,4},{6,7},{7,6},{8,9},{9,8},{10,11... | collective-permute-start | bytes 1572872 | tf_op jit(solution)/shard_map/ppermute | solution.py:356

commit v2 on v1

--- a/solution.py
+++ b/solution.py
@@ -32,31 +32,26 @@
     return jnp.broadcast_to(row, (8, row.shape[1])).T[:, 0:1]
 
 
-def prep_kernel(
-    row0_ref, state_ref, pos_ref, side_ref, value_ref, sigma_ref, noise_ref,
-    x_ref, p_ref, w_ref, hi_scr, lo_scr, m_scr, noise_scr, sem,
+def halves(v):
+    high = v.astype(BF16).astype(F32)
+    return high, v - high
+
+
+def anomaly_kernel(
+    row0_ref, state_ref, pos_ref, side_ref, value_ref, sigma_ref, x_ref, a_ref, hi_scr, m_scr
 ):
     r = pl.program_id(0)
-    fetch = pltpu.make_async_copy(noise_ref, noise_scr, sem)
-
-    @pl.when(r == 0)
-    def _():
-        fetch.start()
-
     s = state_ref[...]
     ms = jnp.mean(s, axis=1, keepdims=True)
     sd = s - ms
     x_ref[...] = sd.astype(BF16)
     dev = 0.5 * (sd + pltpu.roll(sd, WIDTH - 1, 0))
-    hi = dev.astype(BF16)
     here = pl.ds(pl.multiple_of(r * WIDTH, WIDTH), WIDTH)
-    hi_scr[here, :] = hi
-    lo_scr[here, :] = (dev - hi.astype(F32)).astype(BF16)
+    hi_scr[here, :] = dev.astype(BF16)
     mw = jnp.broadcast_to(ms, (WIDTH, 128))
     pm = 0.5 * (mw + pltpu.roll(mw, WIDTH - 1, 0))
-    p0 = pm.astype(BF16).astype(F32)
-    p1 = (pm - p0).astype(BF16).astype(F32)
-    p2 = pm - p0 - p1
+    p0, rest = halves(pm)
+    p1, p2 = halves(rest)
     lane = lax.broadcasted_iota(jnp.int32, (WIDTH, 128), 1)
     m_scr[here, :] = jnp.where(
         lane == 0, p0, jnp.where(lane == 1, p1, jnp.where(lane == 2, p2, 0.0))
@@ -67,64 +62,66 @@
         local = pos_ref[0:1, :] - row0_ref[0]
         col = pos_ref[1:2, :]
         left = (col + side_ref[...] - 1) & (WIDTH - 1)
+        index = column((local * WIDTH + left).astype(F32)).astype(jnp.int32)
+        cells = lax.broadcasted_iota(jnp.int32, (OBS, CELLS), 1)
+        pick = jnp.where(cells == index, 1.0, 0.0).astype(BF16)
+        square = jnp.zeros((OBS, 128), F32)
+        for b in range(4):
+            part = slice(b * 256, (b + 1) * 256)
+            a = jnp.dot(pick, hi_scr[:, part], preferred_element_type=F32)
+            a_ref[0:OBS, part] = a.astype(BF16)
+            square = square + a[:, 0:128] * a[:, 0:128] + a[:, 128:256] * a[:, 128:256]
+        mean = jnp.dot(pick, m_scr[...], preferred_element_type=F32)
+        lane_o = lax.broadcasted_iota(jnp.int32, (OBS, 128), 1)
+        both = jnp.where(
+            lane_o == 0,
+            jnp.sum(mean, axis=1, keepdims=True),
+            jnp.sum(square, axis=1, keepdims=True),
+        ).T
+        sigma = sigma_ref[...]
+        scale = 1.0 / (both[1:2, :] * (1.0 / (M - 1)) + sigma * sigma)
+        lines = [local.astype(F32), col.astype(F32)]
+        for v in (value_ref[...] - both[0:1, :], sigma, scale):
+            lines.extend(halves(v))
         sub = lax.broadcasted_iota(jnp.int32, (16, OBS), 0)
-        code = jnp.where(sub == 0, local.astype(F32), jnp.where(sub == 1, col.astype(F32), 0.0))
-        p_ref[OBS : OBS + 16, 0:OBS] = code.astype(BF16)
-        p_ref[OBS : OBS + 16, OBS:M] = jnp.zeros((16, M - OBS), BF16)
-        index = column((local * WIDTH + left).astype(F32)).astype(jnp.int32)
-        value = column(value_ref[...])
-        sigma = column(sigma_ref[...])
-        fetch.wait()
-        for b in range(4):
-            obs = slice(b * 128, (b + 1) * 128)
-            cells = lax.broadcasted_iota(jnp.int32, (128, CELLS), 1)
-            pick = jnp.where(cells == index[obs], 1.0, 0.0).astype(BF16)
-            high = jnp.dot(pick, hi_scr[...], preferred_element_type=F32)
-            low = jnp.dot(pick, lo_scr[...], preferred_element_type=F32)
-            p_ref[obs, :] = high.astype(BF16)
-            dev_o = high + low
-            mg = jnp.dot(pick, m_scr[...], preferred_element_type=F32)
-            base = value[obs] - jnp.sum(mg, axis=1, keepdims=True)
-            spread = jnp.sum(dev_o * dev_o, axis=1, keepdims=True) * (1.0 / (M - 1))
-            scale = 1.0 / (spread + sigma[obs] * sigma[obs])
-            w = (base + sigma[obs] * noise_scr[obs, :] - dev_o) * scale
-            w_ref[obs, :] = w.astype(BF16)
-
-
-def prep(row0, state, pos, side, value, sigma, noise):
+        code = jnp.zeros((16, OBS), F32)
+        for i, line in enumerate(lines):
+            code = jnp.where(sub == i, line, code)
+        a_ref[OBS : OBS + 16, 0:OBS] = code.astype(BF16)
+        a_ref[OBS : OBS + 16, OBS:M] = jnp.zeros((16, M - OBS), BF16)
+
+
+def anomalies(row0, state, pos, side, value, sigma):
     full = lambda shape: pl.BlockSpec(shape, lambda r: (0,) * len(shape))
     tile = pl.BlockSpec((WIDTH, M), lambda r: (r, 0))
     return pl.pallas_call(
-        prep_kernel,
+        anomaly_kernel,
         grid=(ROWS,),
-        in_specs=[
-            pl.BlockSpec(memory_space=pltpu.SMEM),
-            tile,
-            full((2, OBS)),
-            full((1, OBS)),
-            full((1, OBS)),
-            full((1, OBS)),
-            pl.BlockSpec(memory_space=pl.ANY),
-        ],
-        out_specs=[tile, full((OBS + 16, M)), full((OBS, M))],
+        in_specs=[pl.BlockSpec(memory_space=pltpu.SMEM), tile, full((2, OBS))]
+        + [full((1, OBS))] * 3,
+        out_specs=[tile, full((OBS + 16, M))],
         out_shape=[
             jax.ShapeDtypeStruct((CELLS, M), BF16),
             jax.ShapeDtypeStruct((OBS + 16, M), BF16),
-            jax.ShapeDtypeStruct((OBS, M), BF16),
         ],
-        scratch_shapes=[
-            pltpu.VMEM((CELLS, M), BF16),
-            pltpu.VMEM((CELLS, M), BF16),
-            pltpu.VMEM((CELLS, 128), BF16),
-            pltpu.VMEM((OBS, M), F32),
-            pltpu.SemaphoreType.DMA,
-        ],
+        scratch_shapes=[pltpu.VMEM((CELLS, M), BF16), pltpu.VMEM((CELLS, 128), BF16)],
         compiler_params=pltpu.CompilerParams(
             vmem_limit_bytes=PREP_VMEM, dimension_semantics=("arbitrary",)
         ),
         cost_estimate=cost(1 << 20, 1 << 16),
-        name="prep",
-    )(row0, state, pos, side, value, sigma, noise)
+        name="anomalies",
+    )(row0, state, pos, side, value, sigma)
+
+
+def weights(a_ref, n_ref, w_ref):
+    code = a_ref[OBS : OBS + 16, 0:OBS].astype(F32).T
+    base = code[:, 2:3] + code[:, 3:4]
+    sigma = code[:, 4:5] + code[:, 5:6]
+    scale = code[:, 6:7] + code[:, 7:8]
+    for i in range(OBS // 32):
+        rows = slice(i * 32, (i + 1) * 32)
+        w = base[rows] + sigma[rows] * n_ref[rows, :].astype(F32) - a_ref[rows, :].astype(F32)
+        w_ref[rows, :] = (w * scale[rows]).astype(BF16)
 
 
 def covariance(x, a_ref, cov_ref):
@@ -165,8 +162,11 @@
 def contribute_kernel(distances, sign_ref, x_ref, *refs):
     n = len(distances)
     a_refs = refs[0:n]
-    w_refs = refs[n : 2 * n]
-    acc_ref, out_ref, cov_scr, g_scr = refs[2 * n :]
+    n_refs = refs[n : 2 * n]
+    add_refs = refs[2 * n : -4]
+    out_ref, cov_scr, g_scr, w_scr = refs[-4:]
+    for k in range(n):
+        weights(a_refs[k], n_refs[k], w_scr.at[k])
 
     @pl.loop(0, ROWS)
     def _(r):
@@ -177,27 +177,31 @@
             gain_rows(r, a_refs[k], sign_ref[0] * distance, cov_scr.at[k], g_scr.at[k])
         for h in range(2):
             part = slice(h * (M // 2), (h + 1) * (M // 2))
-            total = acc_ref[here, part]
+            terms = [ref[here, part] for ref in add_refs]
             for k in range(n):
-                total = total + jnp.dot(
-                    g_scr[k], w_refs[k][:, part], preferred_element_type=F32
+                terms.append(
+                    jnp.dot(g_scr[k], w_scr[k, :, part], preferred_element_type=F32)
                 )
-            out_ref[here, part] = total
-
-
-def contribute(sign, x, packets, distances, acc, first=False):
+            out_ref[here, part] = functools.reduce(jnp.add, terms)
+
+
+def contribute(sign, x, packets, distances, *add):
     n = len(distances)
     return pl.pallas_call(
         functools.partial(contribute_kernel, distances),
-        in_specs=[in_smem()] + [in_vmem()] * (2 * n + 2),
+        in_specs=[in_smem()] + [in_vmem()] * (2 * n + 1 + len(add)),
         out_specs=in_vmem(),
         out_shape=jax.ShapeDtypeStruct((CELLS, M), F32),
-        scratch_shapes=[pltpu.VMEM((n, WIDTH, OBS), F32), pltpu.VMEM((n, WIDTH, OBS), BF16)],
-        input_output_aliases={} if first else {2 + 2 * n: 0},
+        scratch_shapes=[
+            pltpu.VMEM((n, WIDTH, OBS), F32),
+            pltpu.VMEM((n, WIDTH, OBS), BF16),
+            pltpu.VMEM((n, OBS, M), BF16),
+        ],
+        input_output_aliases={2 + 2 * n: 0} if add else {},
         compiler_params=params(),
         cost_estimate=cost(1 << 20, 1 << 16),
         name="contribute",
-    )(sign, x, *[a for a, _ in packets], *[w for _, w in packets], acc)
+    )(sign, x, *[a for a, _ in packets], *[n for _, n in packets], *add)
 
 
 def gain_kernel(distance, sign_ref, x_ref, a_ref, g_ref, cov_scr):
@@ -221,7 +225,8 @@
     )(sign, x, a)
 
 
-def edge_kernel(sign_ref, acc_ref, g_ref, w_ref, out_ref, cross_ref, inner_ref):
+def edge_kernel(sign_ref, acc_ref, g_ref, a_ref, n_ref, out_ref, cross_ref, inner_ref, w_ref):
+    weights(a_ref, n_ref, w_ref)
     for i in range(2):
         here = slice(3 * i * WIDTH, (3 * i + 1) * WIDTH)
         for h in range(4):
@@ -241,21 +246,22 @@
                 cross_ref[:, part] = total.astype(BF16)
 
 
-def edges(sign, acc, gain, w):
+def edges(sign, acc, gain, a, noise):
     return pl.pallas_call(
         edge_kernel,
-        in_specs=[in_smem(), in_vmem(), in_vmem(), in_vmem()],
-        out_specs=[in_vmem()] * 3,
+        in_specs=[in_smem()] + [in_vmem()] * 4,
+        out_specs=[in_vmem()] * 4,
         out_shape=[
             jax.ShapeDtypeStruct((CELLS, M), F32),
             jax.ShapeDtypeStruct((WIDTH, M), BF16),
             jax.ShapeDtypeStruct((WIDTH, M), BF16),
+            jax.ShapeDtypeStruct((OBS, M), BF16),
         ],
         input_output_aliases={1: 0},
         compiler_params=params(),
         cost_estimate=cost(1 << 20, 1 << 16),
         name="edges",
-    )(sign, acc, gain, w)
+    )(sign, acc, gain, a, noise)
 
 
 def advance(a, above, below):
@@ -358,28 +364,32 @@
     row0 = (device * ROWS).astype(jnp.int32).reshape(1)
     sign = (2 * (device % 2) - 1).astype(jnp.int32).reshape(1)
     row = lambda v: v.reshape(1, OBS)
-    x, own_a, own_w = prep(
-        row0, state, obs_pos, row(obs_side), row(obs_value), row(obs_sigma), obs_noise
+    own_n, held = lax.optimization_barrier((obs_noise.astype(BF16), state))
+    x, own_a = anomalies(
+        row0, held, obs_pos, row(obs_side), row(obs_value), row(obs_sigma)
     )
 
-    one_a, one_w = beyond(own_a), beyond(own_w)
-    twin_a, twin_w = inside(own_a), inside(own_w)
-    two_a, two_w = beyond(twin_a), beyond(twin_w)
-    acc = contribute(sign, x, ((own_a, own_w), (twin_a, twin_w)), (0, -1), state, True)
-    one_a, acc = hold(one_a, acc)
-    one_twin_a, one_twin_w = inside(one_a), inside(one_w)
-    three_a, three_w = beyond(one_twin_a), beyond(one_twin_w)
-    acc = contribute(sign, x, ((one_a, one_w), (one_twin_a, one_twin_w)), (1, -2), acc)
-    two_a, acc = hold(two_a, acc)
-    two_twin_a, two_twin_w = inside(two_a), inside(two_w)
-    four_a, four_w = beyond(two_twin_a), beyond(two_twin_w)
-    acc = contribute(sign, x, ((two_a, two_w), (two_twin_a, two_twin_w)), (2, -3), acc)
-    three_a, acc = hold(three_a, acc)
-    three_twin_a, three_twin_w = inside(three_a), inside(three_w)
-    acc = contribute(sign, x, ((three_a, three_w), (three_twin_a, three_twin_w)), (3, -4), acc)
+    one_n, one_a = beyond(own_n), beyond(own_a)
+    twin_n, twin_a = inside(own_n), inside(own_a)
+    two_a, two_n = beyond(twin_a), beyond(twin_n)
+    acc = contribute(sign, x, ((own_a, own_n), (twin_a, twin_n)), (0, -1))
+    one_twin_n = inside(one_n)
+    one_a, acc, one_twin_n = lax.optimization_barrier((one_a, acc, one_twin_n))
+    one_twin_a = inside(one_a)
+    one_twin_a, two_a = hold(one_twin_a, two_a)
+    three_a, three_n = beyond(one_twin_a), beyond(one_twin_n)
+    acc = contribute(sign, x, ((one_a, one_n), (one_twin_a, one_twin_n)), (1, -2), acc, state)
+    two_n, acc = hold(two_n, acc)
+    two_twin_a, two_twin_n = inside(two_a), inside(two_n)
+    two_twin_a, three_a = hold(two_twin_a, three_a)
+    four_a, four_n = beyond(two_twin_a), beyond(two_twin_n)
+    acc = contribute(sign, x, ((two_a, two_n), (two_twin_a, two_twin_n)), (2, -3), acc)
+    three_n, acc = hold(three_n, acc)
+    three_twin_a, three_twin_n = inside(three_a), inside(three_n)
+    acc = contribute(sign, x, ((three_a, three_n), (three_twin_a, three_twin_n)), (3, -4), acc)
     four_a, acc = hold(four_a, acc)
     gain = gains(sign, x, four_a, 4)
-    acc, to_cross, to_inner = edges(sign, acc, gain, four_w)
+    acc, to_cross, to_inner, four_w = edges(sign, acc, gain, four_a, four_n)
     cross, inner = beyond(to_cross), inside(to_inner)
     mid, out = middle(acc, gain, four_w)
     return outer(sign, acc, mid, cross, inner, out)

time: 133 us -> 130 us (0.977)
  starting transfers between devices: 41.4 us -> 33.1 us
  Pallas kernels: 55.3 us -> 60.9 us
  local copies, waits for them, and re-layouts: 6.25 us -> 2.83 us
  other arithmetic: 0 us -> 1.75 us
    ppermute x9, starting transfers between devices: 41 us -> 32.9 us  [on_device(): beyond = lambda block: lax.ppermute(block, 'space', across)]
    pallas_call x4, Pallas kernels: 35 us -> 42.2 us  [contribute(): pl.pallas_call(functools.partial(contribute_kernel, distances), in_specs=...]
    unnamed x10 -> x8, local copies, waits for them, and re-layouts: 6.25 us -> 2.83 us
    ppermute x9, waiting for transfers between devices: 27.3 us -> 30.3 us  [on_device(): beyond = lambda block: lax.ppermute(block, 'space', across)]
    ppermute x9, waiting for transfers between devices: 2.38 us -> 0.02 us  [on_device(): inside = lambda block: lax.ppermute(block, 'space', pairs)]
    convert_element_type x0 -> x1, other arithmetic: none -> 1.75 us  [on_device(): own_n, held = lax.optimization_barrier((obs_noise.astype(BF16), state))]
    pallas_call x2, Pallas kernels: 12 us -> 10.4 us  [the longest x1 7.35 us: anomalies(): pl.pallas_call(anomaly_kernel, grid=(ROWS,), in_specs=[pl.BlockSpec(memor...]
  transfers between devices with their start and end apart: 18 -> 18, of which waited for: 6 -> 6; matrix products, arithmetic and copies ran while one was open for 0% -> 0% of each run, Pallas kernels for 31% -> 43%
where the time goes in v2:
time: 130 us; the launch traced here: 129 us
  Pallas kernels  60.9 us (47%)
  starting transfers between devices  33.1 us (25%)
  waiting for transfers between devices  30.3 us (23%)
  local copies, waits for them, and re-layouts  2.83 us (2%)
  other arithmetic  1.75 us (1%)
    pallas_call x4, Pallas kernels, contribute(): pl.pallas_call(functools.partial(contribute_kernel, distances), in_specs=...  42.2 us
    ppermute x9, starting transfers between devices, on_device(): beyond = lambda block: lax.ppermute(block, 'space', across)  32.9 us
    ppermute x9, waiting for transfers between devices, on_device(): beyond = lambda block: lax.ppermute(block, 'space', across)  30.3 us
    pallas_call x1, Pallas kernels, anomalies(): pl.pallas_call(anomaly_kernel, grid=(ROWS,), in_specs=[pl.BlockSpec(memor...  7.35 us
    pallas_call x1, Pallas kernels, gains(): pl.pallas_call(functools.partial(gain_kernel, distance), in_specs=[in_sme...  3.38 us
    pallas_call x1, Pallas kernels, edges(): pl.pallas_call(edge_kernel, in_specs=[in_smem()] + [in_vmem()] * 4, out_s...  3.04 us
    unnamed x8, local copies, waits for them, and re-layouts  2.83 us
    pallas_call x1, Pallas kernels, middle(): pl.pallas_call(middle_kernel, in_specs=[in_vmem()] * 3, out_specs=[in_vme...  2.62 us
  transfers between devices with their start and end apart: 18, of which 6 were waited for; matrix products, arithmetic and copies ran while one was open for 0% of the time, Pallas kernels for 43%

profile of v2, /device:TPU:0, one launch (start us, length us, event | category | flops | bytes accessed | tf_op | source)
XLA Modules:
  0.0 129.2 jit_solution(14034326779665254718)
XLA Ops:
  0.0 1.7 %convert_element_type.3.refs_2_ = bf16[512,1024]{1,0:T(8,128)(2,1)S(1)} convert(f32[512,1024]{1,0:T(8,128)} %param.9) | non-fusion elementwise | flops 524288 | bytes 3145728 | tf_op jit(solution)/shard_map/convert_element_type | solution.py:367
  1.8 8.3 %collective-permute-start.3 = (bf16[512,1024]{1,0:T(8,128)(2,1)S(1)}, bf16[512,1024]{1,0:T(8,128)(2,1)}, u32[]{:S(2)}, u32[]{:S(2)}) collective-permute-start(bf16[512,1024]{1,0:T(8,128)(2,1)S(1)} %convert_element_type.3.refs_2_), channel_id=1, source_target_pairs={{0,127},{1,2},{2,1},{3,4},{4,3},{5,6},{6,5},{7,8},{8,7},{9,10},{10... | collective-permute-start | bytes 3145736 | tf_op jit(solution)/shard_map/ppermute | solution.py:363
  10.0 7.3 %anomalies.1 = (bf16[1024,1024]{1,0:T(8,128)(2,1)}, bf16[528,1024]{1,0:T(8,128)(2,1)}) custom-call(s32[1]{0:T(128)} %bitcast.1.row0_ref, f32[1024,1024]{1,0:T(8,128)} %refs_5_.1, s32[2,512]{1,0:T(2,128)} %pos_ref.1, s32[1,512]{1,0:T(1,128)} %bitcast.5, f32[1,512]{1,0:T(1,128)} %bitcast.6, f32[1,512]{1,0:T(1,128)} %bitcast.7), custom_call_target="tpu_custom_call" | custom-call | flops 1048576 | bytes 65536 | tf_op jit(solution)/shard_map/anomalies/pallas_call | solution.py:97
  17.4 0.7 collective-permute-start
  18.1 0.0 collective-permute-start.2
  18.1 4.5 %collective-permute-done.3.refs_2_ = bf16[512,1024]{1,0:T(8,128)(2,1)} collective-permute-done((bf16[512,1024]{1,0:T(8,128)(2,1)S(1)}, bf16[512,1024]{1,0:T(8,128)(2,1)}, u32[]{:S(2)}, u32[]{:S(2)}) %collective-permute-start.3) | collective-permute-done | bytes 1048608 | tf_op jit(solution)/shard_map/ppermute | solution.py:363
  22.6 7.2 %collective-permute-start.6 = (bf16[528,1024]{1,0:T(8,128)(2,1)S(1)}, bf16[528,1024]{1,0:T(8,128)(2,1)S(1)}, u32[]{:S(2)}, u32[]{:S(2)}) collective-permute-start(bf16[528,1024]{1,0:T(8,128)(2,1)S(1)} %collective-permute-done.1.refs_1_), channel_id=1, source_target_pairs={{0,127},{1,2},{2,1},{3,4},{4,3},{5,6},{6,5},{7,8},{8,7},{9,10},{10... | collective-permute-start | bytes 3244040 | tf_op jit(solution)/shard_map/ppermute | solution.py:363
  29.8 1.6 %copy-done = bf16[1024,1024]{1,0:T(8,128)(2,1)S(1)} copy-done((bf16[1024,1024]{1,0:T(8,128)(2,1)S(1)}, bf16[1024,1024]{1,0:T(8,128)(2,1)}, u32[]{:S(2)}) %copy-start) | copy-done | bytes 2097176
  31.4 1.2 copy-done.3
  32.6 11.3 %contribute.4.refs_4_ = f32[1024,1024]{1,0:T(8,128)S(1)} custom-call(s32[1]{0:T(128)} %bitcast.sign_ref, bf16[1024,1024]{1,0:T(8,128)(2,1)S(1)} %copy-done, bf16[528,1024]{1,0:T(8,128)(2,1)S(1)} %copy-done.3, bf16[528,1024]{1,0:T(8,128)(2,1)S(1)} %collective-permute-done.1.refs_1_, bf16[512,1024]{1,0:T(8,128)(2,1)S(1)} %convert_element_type.3.refs_2_, ...), custom_call_target="tpu_custom_call" | custom-call | flops 1048576 | bytes 65536 | tf_op jit(solution)/shard_map/contribute/pallas_call | solution.py:190
  43.9 0.0 collective-permute-done.refs_0_
  43.9 0.1 collective-permute-start.5
  44.0 0.5 collective-permute-start.12
  44.5 4.7 %collective-permute-done.6.refs_0_ = bf16[528,1024]{1,0:T(8,128)(2,1)S(1)} collective-permute-done((bf16[528,1024]{1,0:T(8,128)(2,1)S(1)}, bf16[528,1024]{1,0:T(8,128)(2,1)S(1)}, u32[]{:S(2)}, u32[]{:S(2)}) %collective-permute-start.6) | collective-permute-done | bytes 1081376 | tf_op jit(solution)/shard_map/ppermute | solution.py:363
  49.3 3.6 %collective-permute-start.8 = (bf16[528,1024]{1,0:T(8,128)(2,1)S(1)}, bf16[528,1024]{1,0:T(8,128)(2,1)S(1)}, u32[]{:S(2)}, u32[]{:S(2)}) collective-permute-start(bf16[528,1024]{1,0:T(8,128)(2,1)S(1)} %collective-permute-done.5.refs_1_), channel_id=1, source_target_pairs={{0,127},{1,2},{2,1},{3,4},{4,3},{5,6},{6,5},{7,8},{8,7},{9,10},{10... | collective-permute-start | bytes 3244040 | tf_op jit(solution)/shard_map/ppermute | solution.py:363
  52.9 11.6 %contribute.5.refs_4_ = f32[1024,1024]{1,0:T(8,128)S(1)} custom-call(s32[1]{0:T(128)} %bitcast.sign_ref, bf16[1024,1024]{1,0:T(8,128)(2,1)S(1)} %copy-done.1, bf16[528,1024]{1,0:T(8,128)(2,1)} %collective-permute-done.refs_0_, bf16[528,1024]{1,0:T(8,128)(2,1)S(1)} %collective-permute-done.5.refs_1_, ...), custom_call_target="tpu_custom_call", output_to_operand_aliasing={{}: (6, {})} | custom-call | flops 1048576 | bytes 65536 | tf_op jit(solution)/shard_map/contribute/pallas_call | solution.py:190
  64.5 0.1 collective-permute-start.13
  64.6 3.7 %collective-permute-start.11 = (bf16[512,1024]{1,0:T(8,128)(2,1)}, bf16[512,1024]{1,0:T(8,128)(2,1)S(1)}, u32[]{:S(2)}, u32[]{:S(2)}) collective-permute-start(bf16[512,1024]{1,0:T(8,128)(2,1)} %collective-permute-done.4.refs_3_), channel_id=1, source_target_pairs={{0,127},{1,2},{2,1},{3,4},{4,3},{5,6},{6,5},{7,8},{8,7},{9,10},{10... | collective-permute-start | bytes 3145736 | tf_op jit(solution)/shard_map/ppermute | solution.py:363
  68.2 7.3 %collective-permute-done.8.refs_0_ = bf16[528,1024]{1,0:T(8,128)(2,1)S(1)} collective-permute-done((bf16[528,1024]{1,0:T(8,128)(2,1)S(1)}, bf16[528,1024]{1,0:T(8,128)(2,1)S(1)}, u32[]{:S(2)}, u32[]{:S(2)}) %collective-permute-start.8) | collective-permute-done | bytes 1081376 | tf_op jit(solution)/shard_map/ppermute | solution.py:363
  75.6 0.4 collective-permute-start.9
  76.0 9.7 %contribute.6.refs_4_ = f32[1024,1024]{1,0:T(8,128)S(1)} custom-call(s32[1]{0:T(128)} %bitcast.sign_ref, bf16[1024,1024]{1,0:T(8,128)(2,1)S(1)} %copy-done.1, bf16[528,1024]{1,0:T(8,128)(2,1)S(1)} %collective-permute-done.6.refs_0_, bf16[528,1024]{1,0:T(8,128)(2,1)S(1)} %collective-permute-done.7.refs_1_, ...), custom_call_target="tpu_custom_call", output_to_operand_aliasing={{}: (6, {})} | custom-call | flops 1048576 | bytes 65536 | tf_op jit(solution)/shard_map/contribute/pallas_call | solution.py:190
  85.7 1.1 collective-permute-done.11.refs_2_
  86.8 5.8 %collective-permute-start.15 = (bf16[512,1024]{1,0:T(8,128)(2,1)S(1)}, bf16[512,1024]{1,0:T(8,128)(2,1)S(1)}, u32[]{:S(2)}, u32[]{:S(2)}) collective-permute-start(bf16[512,1024]{1,0:T(8,128)(2,1)S(1)} %collective-permute-done.13.refs_3_), channel_id=1, source_target_pairs={{0,127},{1,2},{2,1},{3,4},{4,3},{5,6},{6,5},{7,8},{8,7},{9,10},{10... | collective-permute-start | bytes 3145736 | tf_op jit(solution)/shard_map/ppermute | solution.py:363
  92.7 9.7 %contribute.7.acc_ref = f32[1024,1024]{1,0:T(8,128)S(1)} custom-call(s32[1]{0:T(128)} %bitcast.sign_ref, bf16[1024,1024]{1,0:T(8,128)(2,1)S(1)} %copy-done.1, bf16[528,1024]{1,0:T(8,128)(2,1)S(1)} %collective-permute-done.8.refs_0_, bf16[528,1024]{1,0:T(8,128)(2,1)S(1)} %collective-permute-done.10.refs_1_, ...), custom_call_target="tpu_custom_call", output_to_operand_aliasing={{}: (6, {})} | custom-call | flops 1048576 | bytes 65536 | tf_op jit(solution)/shard_map/contribute/pallas_call | solution.py:190
  102.4 3.4 %gains.1.g_ref = bf16[1024,512]{1,0:T(8,128)(2,1)S(1)} custom-call(s32[1]{0:T(128)} %bitcast.sign_ref, bf16[1024,1024]{1,0:T(8,128)(2,1)S(1)} %copy-done.1, bf16[528,1024]{1,0:T(8,128)(2,1)S(1)} %collective-permute-done.9.a_ref), custom_call_target="tpu_custom_call" | custom-call | flops 1048576 | bytes 65536 | tf_op jit(solution)/shard_map/gains/pallas_call | solution.py:216
  105.7 3.9 %collective-permute-done.15.n_ref = bf16[512,1024]{1,0:T(8,128)(2,1)S(1)} collective-permute-done((bf16[512,1024]{1,0:T(8,128)(2,1)S(1)}, bf16[512,1024]{1,0:T(8,128)(2,1)S(1)}, u32[]{:S(2)}, u32[]{:S(2)}) %collective-permute-start.15) | collective-permute-done | bytes 1048608 | tf_op jit(solution)/shard_map/ppermute | solution.py:363
  109.6 3.0 %edges.1 = (f32[1024,1024]{1,0:T(8,128)S(1)}, bf16[256,1024]{1,0:T(8,128)(2,1)S(1)}, bf16[256,1024]{1,0:T(8,128)(2,1)S(1)}, bf16[512,1024]{1,0:T(8,128)(2,1)S(1)}) custom-call(s32[1]{0:T(128)} %bitcast.sign_ref, f32[1024,1024]{1,0:T(8,128)S(1)} %contribute.7.acc_ref, bf16[1024,512]{1,0:T(8,128)(2,1)S(1)} %gains.1.g_ref, ...), custom_call_target="tpu_custom_call", output_to_operand_aliasing={{0}: (1, {})} | custom-call | flops 1048576 | bytes 65536 | tf_op jit(solution)/shard_map/edges/pallas_call | solution.py:250
  112.7 2.8 %collective-permute-start.16 = (bf16[256,1024]{1,0:T(8,128)(2,1)S(1)}, bf16[256,1024]{1,0:T(8,128)(2,1)S(1)}, u32[]{:S(2)}, u32[]{:S(2)}) collective-permute-start(bf16[256,1024]{1,0:T(8,128)(2,1)S(1)} %get-tuple-element.48), channel_id=1, source_target_pairs={{0,127},{1,2},{2,1},{3,4},{4,3},{5,6},{6,5},{7,8},{8,7},{9,10},{10... | collective-permute-start | bytes 1572872 | tf_op jit(solution)/shard_map/ppermute | solution.py:363
  115.4 0.0 collective-permute-start.17
  115.4 2.6 %middle.1 = (f32[512,1024]{1,0:T(8,128)S(1)}, f32[1024,1024]{1,0:T(8,128)}) custom-call(f32[1024,1024]{1,0:T(8,128)S(1)} %get-tuple-element.45.acc_ref, bf16[1024,512]{1,0:T(8,128)(2,1)S(1)} %gains.1.g_ref, bf16[512,1024]{1,0:T(8,128)(2,1)S(1)} %get-tuple-element.46.w_ref), custom_call_target="tpu_custom_call" | custom-call | flops 1048576 | bytes 65536 | tf_op jit(solution)/shard_map/middle/pallas_call | solution.py:300
  118.1 8.7 %collective-permute-done.16.cross_ref = bf16[256,1024]{1,0:T(8,128)(2,1)S(1)} collective-permute-done((bf16[256,1024]{1,0:T(8,128)(2,1)S(1)}, bf16[256,1024]{1,0:T(8,128)(2,1)S(1)}, u32[]{:S(2)}, u32[]{:S(2)}) %collective-permute-start.16) | collective-permute-done | bytes 524320 | tf_op jit(solution)/shard_map/ppermute | solution.py:363
  126.8 2.2 %outer.1 = f32[1024,1024]{1,0:T(8,128)} custom-call(s32[1]{0:T(128)} %bitcast.sign_ref, f32[1024,1024]{1,0:T(8,128)S(1)} %get-tuple-element.45.acc_ref, f32[512,1024]{1,0:T(8,128)S(1)} %get-tuple-element.47.mid_ref, bf16[256,1024]{1,0:T(8,128)(2,1)S(1)} %collective-permute-done.16.cross_ref, ...), custom_call_target="tpu_custom_call", output_to_operand_aliasing={{}: (5, {})} | custom-call | flops 1048576 | bytes 65536 | tf_op jit(solution)/shard_map/outer/pallas_call | solution.py:339
  (22 shorter events, 0.1 us)
Async XLA Ops:
  1.8 20.9 %collective-permute-start.3 = (bf16[512,1024]{1,0:T(8,128)(2,1)S(1)}, bf16[512,1024]{1,0:T(8,128)(2,1)}, u32[]{:S(2)}, u32[]{:S(2)}) collective-permute-start(bf16[512,1024]{1,0:T(8,128)(2,1)S(1)} %convert_element_type.3.refs_2_), channel_id=1, source_target_pairs={{0,127},{1,2},{2,1},{3,4},{4,3},{5,6},{6,5},{7,8},{8,7},{9,10},{10... | collective-permute-start | bytes 3145736 | tf_op jit(solution)/shard_map/ppermute | solution.py:363
  17.4 5.2 %collective-permute-start.1 = (bf16[528,1024]{1,0:T(8,128)(2,1)}, bf16[528,1024]{1,0:T(8,128)(2,1)S(1)}, u32[]{:S(2)}, u32[]{:S(2)}) collective-permute-start(bf16[528,1024]{1,0:T(8,128)(2,1)} %get-tuple-element.29.refs_0_), channel_id=1, source_target_pairs={{0,1},{1,0},{2,3},{3,2},{4,5},{5,4},{6,7},{7,6},{8,9},{9,8},{10,11... | collective-permute-start | bytes 3244040 | tf_op jit(solution)/shard_map/ppermute | solution.py:362
  17.4 26.5 %collective-permute-start = (bf16[528,1024]{1,0:T(8,128)(2,1)}, bf16[528,1024]{1,0:T(8,128)(2,1)}, u32[]{:S(2)}, u32[]{:S(2)}) collective-permute-start(bf16[528,1024]{1,0:T(8,128)(2,1)} %get-tuple-element.29.refs_0_), channel_id=1, source_target_pairs={{0,127},{1,2},{2,1},{3,4},{4,3},{5,6},{6,5},{7,8},{8,7},{9,10},{10... | collective-permute-start | bytes 3244040 | tf_op jit(solution)/shard_map/ppermute | solution.py:363
  18.1 11.7 %collective-permute-start.2 = (bf16[512,1024]{1,0:T(8,128)(2,1)S(1)}, bf16[512,1024]{1,0:T(8,128)(2,1)}, u32[]{:S(2)}, u32[]{:S(2)}) collective-permute-start(bf16[512,1024]{1,0:T(8,128)(2,1)S(1)} %convert_element_type.3.refs_2_), channel_id=1, source_target_pairs={{0,1},{1,0},{2,3},{3,2},{4,5},{5,4},{6,7},{7,6},{8,9},{9,8},{10,11... | collective-permute-start | bytes 3145736 | tf_op jit(solution)/shard_map/ppermute | solution.py:362
  22.6 21.3 %collective-permute-start.4 = (bf16[512,1024]{1,0:T(8,128)(2,1)}, bf16[512,1024]{1,0:T(8,128)(2,1)}, u32[]{:S(2)}, u32[]{:S(2)}) collective-permute-start(bf16[512,1024]{1,0:T(8,128)(2,1)} %collective-permute-done.3.refs_2_), channel_id=1, source_target_pairs={{0,1},{1,0},{2,3},{3,2},{4,5},{5,4},{6,7},{7,6},{8,9},{9,8},{10,11... | collective-permute-start | bytes 3145736 | tf_op jit(solution)/shard_map/ppermute | solution.py:362
  22.6 26.6 %collective-permute-start.6 = (bf16[528,1024]{1,0:T(8,128)(2,1)S(1)}, bf16[528,1024]{1,0:T(8,128)(2,1)S(1)}, u32[]{:S(2)}, u32[]{:S(2)}) collective-permute-start(bf16[528,1024]{1,0:T(8,128)(2,1)S(1)} %collective-permute-done.1.refs_1_), channel_id=1, source_target_pairs={{0,127},{1,2},{2,1},{3,4},{4,3},{5,6},{6,5},{7,8},{8,7},{9,10},{10... | collective-permute-start | bytes 3244040 | tf_op jit(solution)/shard_map/ppermute | solution.py:363
  29.8 1.6 %copy-start = (bf16[1024,1024]{1,0:T(8,128)(2,1)S(1)}, bf16[1024,1024]{1,0:T(8,128)(2,1)}, u32[]{:S(2)}) copy-start(bf16[1024,1024]{1,0:T(8,128)(2,1)} %get-tuple-element.30.x_ref) | copy-start | bytes 6291460
  31.4 1.2 copy-start.3
  32.6 20.2 %copy-start.1 = (bf16[1024,1024]{1,0:T(8,128)(2,1)S(1)}, bf16[1024,1024]{1,0:T(8,128)(2,1)}, u32[]{:S(2)}) copy-start(bf16[1024,1024]{1,0:T(8,128)(2,1)} %get-tuple-element.30.x_ref) | copy-start | bytes 6291460
  32.6 20.2 %copy-start.2 = (f32[1024,1024]{1,0:T(8,128)S(1)}, f32[1024,1024]{1,0:T(8,128)}, u32[]{:S(2)}) copy-start(f32[1024,1024]{1,0:T(8,128)} %refs_5_.1) | copy-start | bytes 12582916
  43.9 5.3 %collective-permute-start.5 = (bf16[528,1024]{1,0:T(8,128)(2,1)}, bf16[528,1024]{1,0:T(8,128)(2,1)S(1)}, u32[]{:S(2)}, u32[]{:S(2)}) collective-permute-start(bf16[528,1024]{1,0:T(8,128)(2,1)} %collective-permute-done.refs_0_), channel_id=1, source_target_pairs={{0,1},{1,0},{2,3},{3,2},{4,5},{5,4},{6,7},{7,6},{8,9},{9,8},{10,11... | collective-permute-start | bytes 3244040 | tf_op jit(solution)/shard_map/ppermute | solution.py:362
  44.0 20.4 %collective-permute-start.12 = (bf16[512,1024]{1,0:T(8,128)(2,1)}, bf16[512,1024]{1,0:T(8,128)(2,1)S(1)}, u32[]{:S(2)}, u32[]{:S(2)}) collective-permute-start(bf16[512,1024]{1,0:T(8,128)(2,1)} %collective-permute-done.2.refs_3_), channel_id=1, source_target_pairs={{0,127},{1,2},{2,1},{3,4},{4,3},{5,6},{6,5},{7,8},{8,7},{9,10},{10... | collective-permute-start | bytes 3145736 | tf_op jit(solution)/shard_map/ppermute | solution.py:363
  49.3 19.0 %collective-permute-start.7 = (bf16[528,1024]{1,0:T(8,128)(2,1)S(1)}, bf16[528,1024]{1,0:T(8,128)(2,1)S(1)}, u32[]{:S(2)}, u32[]{:S(2)}) collective-permute-start(bf16[528,1024]{1,0:T(8,128)(2,1)S(1)} %collective-permute-done.6.refs_0_), channel_id=1, source_target_pairs={{0,1},{1,0},{2,3},{3,2},{4,5},{5,4},{6,7},{7,6},{8,9},{9,8},{10,11... | collective-permute-start | bytes 3244040 | tf_op jit(solution)/shard_map/ppermute | solution.py:362
  49.3 26.3 %collective-permute-start.8 = (bf16[528,1024]{1,0:T(8,128)(2,1)S(1)}, bf16[528,1024]{1,0:T(8,128)(2,1)S(1)}, u32[]{:S(2)}, u32[]{:S(2)}) collective-permute-start(bf16[528,1024]{1,0:T(8,128)(2,1)S(1)} %collective-permute-done.5.refs_1_), channel_id=1, source_target_pairs={{0,127},{1,2},{2,1},{3,4},{4,3},{5,6},{6,5},{7,8},{8,7},{9,10},{10... | collective-permute-start | bytes 3244040 | tf_op jit(solution)/shard_map/ppermute | solution.py:363
  64.5 11.5 %collective-permute-start.13 = (bf16[512,1024]{1,0:T(8,128)(2,1)S(1)}, bf16[512,1024]{1,0:T(8,128)(2,1)S(1)}, u32[]{:S(2)}, u32[]{:S(2)}) collective-permute-start(bf16[512,1024]{1,0:T(8,128)(2,1)S(1)} %collective-permute-done.12.refs_2_), channel_id=1, source_target_pairs={{0,1},{1,0},{2,3},{3,2},{4,5},{5,4},{6,7},{7,6},{8,9},{9,8},{10,11... | collective-permute-start | bytes 3145736 | tf_op jit(solution)/shard_map/ppermute | solution.py:362
  64.6 22.2 %collective-permute-start.11 = (bf16[512,1024]{1,0:T(8,128)(2,1)}, bf16[512,1024]{1,0:T(8,128)(2,1)S(1)}, u32[]{:S(2)}, u32[]{:S(2)}) collective-permute-start(bf16[512,1024]{1,0:T(8,128)(2,1)} %collective-permute-done.4.refs_3_), channel_id=1, source_target_pairs={{0,127},{1,2},{2,1},{3,4},{4,3},{5,6},{6,5},{7,8},{8,7},{9,10},{10... | collective-permute-start | bytes 3145736 | tf_op jit(solution)/shard_map/ppermute | solution.py:363
  75.6 17.1 %collective-permute-start.10 = (bf16[528,1024]{1,0:T(8,128)(2,1)S(1)}, bf16[528,1024]{1,0:T(8,128)(2,1)S(1)}, u32[]{:S(2)}, u32[]{:S(2)}) collective-permute-start(bf16[528,1024]{1,0:T(8,128)(2,1)S(1)} %collective-permute-done.8.refs_0_), channel_id=1, source_target_pairs={{0,1},{1,0},{2,3},{3,2},{4,5},{5,4},{6,7},{7,6},{8,9},{9,8},{10,11... | collective-permute-start | bytes 3244040 | tf_op jit(solution)/shard_map/ppermute | solution.py:362
  75.6 26.8 %collective-permute-start.9 = (bf16[528,1024]{1,0:T(8,128)(2,1)S(1)}, bf16[528,1024]{1,0:T(8,128)(2,1)S(1)}, u32[]{:S(2)}, u32[]{:S(2)}) collective-permute-start(bf16[528,1024]{1,0:T(8,128)(2,1)S(1)} %collective-permute-done.7.refs_1_), channel_id=1, source_target_pairs={{0,127},{1,2},{2,1},{3,4},{4,3},{5,6},{6,5},{7,8},{8,7},{9,10},{10... | collective-permute-start | bytes 3244040 | tf_op jit(solution)/shard_map/ppermute | solution.py:363
  86.8 5.8 %collective-permute-start.14 = (bf16[512,1024]{1,0:T(8,128)(2,1)S(1)}, bf16[512,1024]{1,0:T(8,128)(2,1)S(1)}, u32[]{:S(2)}, u32[]{:S(2)}) collective-permute-start(bf16[512,1024]{1,0:T(8,128)(2,1)S(1)} %collective-permute-done.11.refs_2_), channel_id=1, source_target_pairs={{0,1},{1,0},{2,3},{3,2},{4,5},{5,4},{6,7},{7,6},{8,9},{9,8},{10,11... | collective-permute-start | bytes 3145736 | tf_op jit(solution)/shard_map/ppermute | solution.py:362
  86.8 22.8 %collective-permute-start.15 = (bf16[512,1024]{1,0:T(8,128)(2,1)S(1)}, bf16[512,1024]{1,0:T(8,128)(2,1)S(1)}, u32[]{:S(2)}, u32[]{:S(2)}) collective-permute-start(bf16[512,1024]{1,0:T(8,128)(2,1)S(1)} %collective-permute-done.13.refs_3_), channel_id=1, source_target_pairs={{0,127},{1,2},{2,1},{3,4},{4,3},{5,6},{6,5},{7,8},{8,7},{9,10},{10... | collective-permute-start | bytes 3145736 | tf_op jit(solution)/shard_map/ppermute | solution.py:363
  112.7 14.1 %collective-permute-start.16 = (bf16[256,1024]{1,0:T(8,128)(2,1)S(1)}, bf16[256,1024]{1,0:T(8,128)(2,1)S(1)}, u32[]{:S(2)}, u32[]{:S(2)}) collective-permute-start(bf16[256,1024]{1,0:T(8,128)(2,1)S(1)} %get-tuple-element.48), channel_id=1, source_target_pairs={{0,127},{1,2},{2,1},{3,4},{4,3},{5,6},{6,5},{7,8},{8,7},{9,10},{10... | collective-permute-start | bytes 1572872 | tf_op jit(solution)/shard_map/ppermute | solution.py:363
  115.4 11.4 %collective-permute-start.17 = (bf16[256,1024]{1,0:T(8,128)(2,1)S(1)}, bf16[256,1024]{1,0:T(8,128)(2,1)S(1)}, u32[]{:S(2)}, u32[]{:S(2)}) collective-permute-start(bf16[256,1024]{1,0:T(8,128)(2,1)S(1)} %get-tuple-element.49), channel_id=1, source_target_pairs={{0,1},{1,0},{2,3},{3,2},{4,5},{5,4},{6,7},{7,6},{8,9},{9,8},{10,11... | collective-permute-start | bytes 1572872 | tf_op jit(solution)/shard_map/ppermute | solution.py:362

commit v3 on v2

--- a/solution.py
+++ b/solution.py
@@ -125,30 +125,48 @@
 
 
 def covariance(x, a_ref, cov_ref):
-    cov_ref[...] = lax.dot_general(
-        x, a_ref[0:OBS, :], (((1,), (1,)), ((), ())), preferred_element_type=F32
-    )
-
-
-def gain_rows(r, a_ref, offset, cov_ref, g_ref):
+    for h in range(2):
+        part = slice(h * 256, (h + 1) * 256)
+        cov_ref[:, part] = lax.dot_general(
+            x, a_ref[part, :], (((1,), (1,)), ((), ())), preferred_element_type=F32
+        )
+
+
+def gain_rows(a_ref, offset, cov_ref, g_ref, unroll):
     code = a_ref[OBS : OBS + 16, 0:OBS].astype(F32)
-    gap = jnp.abs(code[0:1, :] + (ROWS * offset - r).astype(F32))
-    row2 = jnp.where(gap > REACH * ROWS, 1e4, jnp.maximum(gap * gap * (1.0 / 256.0), 1e-12))
     col = code[1:2, :] * (1.0 / 16.0)
     n1 = 1.0 / (M - 1)
-    for i in range(WIDTH // CHUNK):
-        rows = slice(i * CHUNK, (i + 1) * CHUNK)
-        q = (lax.broadcasted_iota(jnp.int32, (CHUNK, 1), 0) + i * CHUNK).astype(F32) * (1.0 / 16.0)
-        d = jnp.abs(q - col)
-        d = jnp.minimum(d, 16.0 - d)
-        z2 = d * d + row2
-        inv = lax.rsqrt(z2)
-        z = z2 * inv
-        near = z2 * (z * ((0.625 * n1) + z * ((0.5 * n1) - (0.25 * n1) * z)) - (5.0 / 3.0 * n1)) + n1
-        u = jnp.maximum(2.0 - z, 0.0)
-        u2 = u * u
-        far = (u2 * u2) * ((z2 + (2.0 * z - 0.5)) * (inv * (n1 / 12.0)))
-        g_ref[rows, :] = (jnp.where(z2 <= 1.0, near, far) * cov_ref[rows, :]).astype(BF16)
+    row2 = []
+    for r in range(ROWS):
+        gap = jnp.abs(code[0:1, :] + (ROWS * offset - r).astype(F32))
+        row2.append(
+            jnp.where(gap > REACH * ROWS, 1e4, jnp.maximum(gap * gap * (1.0 / 256.0), 1e-12))
+        )
+
+    @pl.loop(0, WIDTH // CHUNK, unroll=unroll)
+    def _(i):
+        q = lax.broadcasted_iota(jnp.int32, (CHUNK, 1), 0) + i * CHUNK
+        q = q.astype(F32) * (1.0 / 16.0)
+        for h in range(2):
+            part = slice(h * 256, (h + 1) * 256)
+            d = jnp.abs(q - col[:, part])
+            d = jnp.minimum(d, 16.0 - d)
+            d = d * d
+            for r in range(ROWS):
+                rows = pl.ds(pl.multiple_of(r * WIDTH + i * CHUNK, CHUNK), CHUNK)
+                z2 = d + row2[r][:, part]
+                inv = lax.rsqrt(z2)
+                z = z2 * inv
+                near = (
+                    z2 * (z * ((0.625 * n1) + z * ((0.5 * n1) - (0.25 * n1) * z)) - (5.0 / 3.0 * n1))
+                    + n1
+                )
+                u = jnp.maximum(2.0 - z, 0.0)
+                u2 = u * u
+                far = (u2 * u2) * ((z2 + (2.0 * z - 0.5)) * (inv * (n1 / 12.0)))
+                g_ref[rows, part] = (
+                    jnp.where(z2 <= 1.0, near, far) * cov_ref[rows, part]
+                ).astype(BF16)
 
 
 def in_vmem():
@@ -159,7 +177,7 @@
     return pl.BlockSpec(memory_space=pltpu.SMEM)
 
 
-def contribute_kernel(distances, sign_ref, x_ref, *refs):
+def contribute_kernel(distances, unroll, sign_ref, x_ref, *refs):
     n = len(distances)
     a_refs = refs[0:n]
     n_refs = refs[n : 2 * n]
@@ -168,33 +186,28 @@
     for k in range(n):
         weights(a_refs[k], n_refs[k], w_scr.at[k])
 
-    @pl.loop(0, ROWS)
-    def _(r):
-        here = pl.ds(pl.multiple_of(r * WIDTH, WIDTH), WIDTH)
+    for k, distance in enumerate(distances):
+        covariance(x_ref[...], a_refs[k], cov_scr.at[k])
+    for k, distance in enumerate(distances):
+        gain_rows(a_refs[k], sign_ref[0] * distance, cov_scr.at[k], g_scr.at[k], unroll)
+    for h in range(4):
+        part = slice(h * (M // 4), (h + 1) * (M // 4))
+        terms = [ref[:, part] for ref in add_refs]
         for k in range(n):
-            covariance(x_ref[here, :], a_refs[k], cov_scr.at[k])
-        for k, distance in enumerate(distances):
-            gain_rows(r, a_refs[k], sign_ref[0] * distance, cov_scr.at[k], g_scr.at[k])
-        for h in range(2):
-            part = slice(h * (M // 2), (h + 1) * (M // 2))
-            terms = [ref[here, part] for ref in add_refs]
-            for k in range(n):
-                terms.append(
-                    jnp.dot(g_scr[k], w_scr[k, :, part], preferred_element_type=F32)
-                )
-            out_ref[here, part] = functools.reduce(jnp.add, terms)
-
-
-def contribute(sign, x, packets, distances, *add):
+            terms.append(jnp.dot(g_scr[k], w_scr[k, :, part], preferred_element_type=F32))
+        out_ref[:, part] = functools.reduce(jnp.add, terms)
+
+
+def contribute(sign, x, packets, distances, *add, unroll=1):
     n = len(distances)
     return pl.pallas_call(
-        functools.partial(contribute_kernel, distances),
+        functools.partial(contribute_kernel, distances, unroll),
         in_specs=[in_smem()] + [in_vmem()] * (2 * n + 1 + len(add)),
         out_specs=in_vmem(),
         out_shape=jax.ShapeDtypeStruct((CELLS, M), F32),
         scratch_shapes=[
-            pltpu.VMEM((n, WIDTH, OBS), F32),
-            pltpu.VMEM((n, WIDTH, OBS), BF16),
+            pltpu.VMEM((n, CELLS, OBS), F32),
+            pltpu.VMEM((n, CELLS, OBS), BF16),
             pltpu.VMEM((n, OBS, M), BF16),
         ],
         input_output_aliases={2 + 2 * n: 0} if add else {},
@@ -205,11 +218,8 @@
 
 
 def gain_kernel(distance, sign_ref, x_ref, a_ref, g_ref, cov_scr):
-    @pl.loop(0, ROWS)
-    def _(r):
-        here = pl.ds(pl.multiple_of(r * WIDTH, WIDTH), WIDTH)
-        covariance(x_ref[here, :], a_ref, cov_scr)
-        gain_rows(r, a_ref, sign_ref[0] * distance, cov_scr, g_ref.at[here])
+    covariance(x_ref[...], a_ref, cov_scr)
+    gain_rows(a_ref, sign_ref[0] * distance, cov_scr, g_ref, 16)
 
 
 def gains(sign, x, a, distance):
@@ -218,7 +228,7 @@
         in_specs=[in_smem(), in_vmem(), in_vmem()],
         out_specs=in_vmem(),
         out_shape=jax.ShapeDtypeStruct((CELLS, OBS), BF16),
-        scratch_shapes=[pltpu.VMEM((WIDTH, OBS), F32)],
+        scratch_shapes=[pltpu.VMEM((CELLS, OBS), F32)],
         compiler_params=params(),
         cost_estimate=cost(1 << 20, 1 << 16),
         name="gains",
@@ -386,7 +396,8 @@
     acc = contribute(sign, x, ((two_a, two_n), (two_twin_a, two_twin_n)), (2, -3), acc)
     three_n, acc = hold(three_n, acc)
     three_twin_a, three_twin_n = inside(three_a), inside(three_n)
-    acc = contribute(sign, x, ((three_a, three_n), (three_twin_a, three_twin_n)), (3, -4), acc)
+    last = ((three_a, three_n), (three_twin_a, three_twin_n))
+    acc = contribute(sign, x, last, (3, -4), acc, unroll=16)
     four_a, acc = hold(four_a, acc)
     gain = gains(sign, x, four_a, 4)
     acc, to_cross, to_inner, four_w = edges(sign, acc, gain, four_a, four_n)

time: 130 us -> 129 us (level)
  Pallas kernels: 60.9 us -> 57.2 us
  waiting for transfers between devices: 30.3 us -> 33.1 us
    pallas_call x4, Pallas kernels: 42.2 us -> 39.2 us  [contribute(): pl.pallas_call(functools.partial(contribute_kernel, distances, unroll), i...]
    ppermute x9, waiting for transfers between devices: 30.3 us -> 33.1 us  [on_device(): beyond = lambda block: lax.ppermute(block, 'space', across)]
  transfers between devices with their start and end apart: 18 -> 18, of which waited for: 6 -> 6; matrix products, arithmetic and copies ran while one was open for 0% -> 0% of each run, Pallas kernels for 43% -> 40%
where the time goes in v3:
time: 129 us; the launch traced here: 128 us
  Pallas kernels  57.2 us (44%)
  starting transfers between devices  33.2 us (26%)
  waiting for transfers between devices  33.1 us (26%)
  local copies, waits for them, and re-layouts  2.83 us (2%)
  other arithmetic  1.75 us (1%)
    pallas_call x4, Pallas kernels, contribute(): pl.pallas_call(functools.partial(contribute_kernel, distances, unroll), i...  39.2 us
    ppermute x9, waiting for transfers between devices, on_device(): beyond = lambda block: lax.ppermute(block, 'space', across)  33.1 us
    ppermute x9, starting transfers between devices, on_device(): beyond = lambda block: lax.ppermute(block, 'space', across)  33 us
    pallas_call x1, Pallas kernels, anomalies(): pl.pallas_call(anomaly_kernel, grid=(ROWS,), in_specs=[pl.BlockSpec(memor...  7.35 us
    pallas_call x1, Pallas kernels, edges(): pl.pallas_call(edge_kernel, in_specs=[in_smem()] + [in_vmem()] * 4, out_s...  3.04 us
    unnamed x8, local copies, waits for them, and re-layouts  2.83 us
    pallas_call x1, Pallas kernels, gains(): pl.pallas_call(functools.partial(gain_kernel, distance), in_specs=[in_sme...  2.75 us
    pallas_call x1, Pallas kernels, middle(): pl.pallas_call(middle_kernel, in_specs=[in_vmem()] * 3, out_specs=[in_vme...  2.62 us
  transfers between devices with their start and end apart: 18, of which 6 were waited for; matrix products, arithmetic and copies ran while one was open for 0% of the time, Pallas kernels for 40%

profile of v3, /device:TPU:0, one launch (start us, length us, event | category | flops | bytes accessed | tf_op | source)
XLA Modules:
  0.0 128.4 jit_solution(11890254607021809014)
XLA Ops:
  0.0 1.7 %convert_element_type.3.refs_2_ = bf16[512,1024]{1,0:T(8,128)(2,1)S(1)} convert(f32[512,1024]{1,0:T(8,128)} %param.9) | non-fusion elementwise | flops 524288 | bytes 3145728 | tf_op jit(solution)/shard_map/convert_element_type | solution.py:377
  1.8 8.3 %collective-permute-start.3 = (bf16[512,1024]{1,0:T(8,128)(2,1)S(1)}, bf16[512,1024]{1,0:T(8,128)(2,1)}, u32[]{:S(2)}, u32[]{:S(2)}) collective-permute-start(bf16[512,1024]{1,0:T(8,128)(2,1)S(1)} %convert_element_type.3.refs_2_), channel_id=1, source_target_pairs={{0,127},{1,2},{2,1},{3,4},{4,3},{5,6},{6,5},{7,8},{8,7},{9,10},{10... | collective-permute-start | bytes 3145736 | tf_op jit(solution)/shard_map/ppermute | solution.py:373
  10.0 7.3 %anomalies.1 = (bf16[1024,1024]{1,0:T(8,128)(2,1)}, bf16[528,1024]{1,0:T(8,128)(2,1)}) custom-call(s32[1]{0:T(128)} %bitcast.1.row0_ref, f32[1024,1024]{1,0:T(8,128)} %refs_5_.1, s32[2,512]{1,0:T(2,128)} %pos_ref.1, s32[1,512]{1,0:T(1,128)} %bitcast.5, f32[1,512]{1,0:T(1,128)} %bitcast.6, f32[1,512]{1,0:T(1,128)} %bitcast.7), custom_call_target="tpu_custom_call" | custom-call | flops 1048576 | bytes 65536 | tf_op jit(solution)/shard_map/anomalies/pallas_call | solution.py:97
  17.4 0.7 collective-permute-start
  18.1 0.0 collective-permute-start.2
  18.1 4.5 %collective-permute-done.3.refs_2_ = bf16[512,1024]{1,0:T(8,128)(2,1)} collective-permute-done((bf16[512,1024]{1,0:T(8,128)(2,1)S(1)}, bf16[512,1024]{1,0:T(8,128)(2,1)}, u32[]{:S(2)}, u32[]{:S(2)}) %collective-permute-start.3) | collective-permute-done | bytes 1048608 | tf_op jit(solution)/shard_map/ppermute | solution.py:373
  22.6 7.2 %collective-permute-start.6 = (bf16[528,1024]{1,0:T(8,128)(2,1)S(1)}, bf16[528,1024]{1,0:T(8,128)(2,1)S(1)}, u32[]{:S(2)}, u32[]{:S(2)}) collective-permute-start(bf16[528,1024]{1,0:T(8,128)(2,1)S(1)} %collective-permute-done.1.refs_1_), channel_id=1, source_target_pairs={{0,127},{1,2},{2,1},{3,4},{4,3},{5,6},{6,5},{7,8},{8,7},{9,10},{10... | collective-permute-start | bytes 3244040 | tf_op jit(solution)/shard_map/ppermute | solution.py:373
  29.8 1.6 %copy-done = bf16[1024,1024]{1,0:T(8,128)(2,1)S(1)} copy-done((bf16[1024,1024]{1,0:T(8,128)(2,1)S(1)}, bf16[1024,1024]{1,0:T(8,128)(2,1)}, u32[]{:S(2)}) %copy-start) | copy-done | bytes 2097176
  31.4 1.2 copy-done.3
  32.6 10.4 %contribute.4.refs_4_ = f32[1024,1024]{1,0:T(8,128)S(1)} custom-call(s32[1]{0:T(128)} %bitcast.sign_ref, bf16[1024,1024]{1,0:T(8,128)(2,1)S(1)} %copy-done, bf16[528,1024]{1,0:T(8,128)(2,1)S(1)} %copy-done.3, bf16[528,1024]{1,0:T(8,128)(2,1)S(1)} %collective-permute-done.1.refs_1_, bf16[512,1024]{1,0:T(8,128)(2,1)S(1)} %convert_element_type.3.refs_2_, ...), custom_call_target="tpu_custom_call" | custom-call | flops 1048576 | bytes 65536 | tf_op jit(solution)/shard_map/contribute/pallas_call | solution.py:203
  43.1 0.0 collective-permute-done.4.refs_3_
  43.1 0.1 collective-permute-start.5
  43.2 0.5 collective-permute-start.12
  43.7 5.6 %collective-permute-done.6.refs_0_ = bf16[528,1024]{1,0:T(8,128)(2,1)S(1)} collective-permute-done((bf16[528,1024]{1,0:T(8,128)(2,1)S(1)}, bf16[528,1024]{1,0:T(8,128)(2,1)S(1)}, u32[]{:S(2)}, u32[]{:S(2)}) %collective-permute-start.6) | collective-permute-done | bytes 1081376 | tf_op jit(solution)/shard_map/ppermute | solution.py:373
  49.3 3.6 %collective-permute-start.8 = (bf16[528,1024]{1,0:T(8,128)(2,1)S(1)}, bf16[528,1024]{1,0:T(8,128)(2,1)S(1)}, u32[]{:S(2)}, u32[]{:S(2)}) collective-permute-start(bf16[528,1024]{1,0:T(8,128)(2,1)S(1)} %collective-permute-done.5.refs_1_), channel_id=1, source_target_pairs={{0,127},{1,2},{2,1},{3,4},{4,3},{5,6},{6,5},{7,8},{8,7},{9,10},{10... | collective-permute-start | bytes 3244040 | tf_op jit(solution)/shard_map/ppermute | solution.py:373
  52.9 11.8 %contribute.5.refs_4_ = f32[1024,1024]{1,0:T(8,128)S(1)} custom-call(s32[1]{0:T(128)} %bitcast.sign_ref, bf16[1024,1024]{1,0:T(8,128)(2,1)S(1)} %copy-done.1, bf16[528,1024]{1,0:T(8,128)(2,1)} %collective-permute-done.refs_0_, bf16[528,1024]{1,0:T(8,128)(2,1)S(1)} %collective-permute-done.5.refs_1_, ...), custom_call_target="tpu_custom_call", output_to_operand_aliasing={{}: (6, {})} | custom-call | flops 1048576 | bytes 65536 | tf_op jit(solution)/shard_map/contribute/pallas_call | solution.py:203
  64.7 0.1 collective-permute-start.13
  64.8 3.7 %collective-permute-start.11 = (bf16[512,1024]{1,0:T(8,128)(2,1)}, bf16[512,1024]{1,0:T(8,128)(2,1)S(1)}, u32[]{:S(2)}, u32[]{:S(2)}) collective-permute-start(bf16[512,1024]{1,0:T(8,128)(2,1)} %collective-permute-done.4.refs_3_), channel_id=1, source_target_pairs={{0,127},{1,2},{2,1},{3,4},{4,3},{5,6},{6,5},{7,8},{8,7},{9,10},{10... | collective-permute-start | bytes 3145736 | tf_op jit(solution)/shard_map/ppermute | solution.py:373
  68.5 6.2 %collective-permute-done.8.refs_0_ = bf16[528,1024]{1,0:T(8,128)(2,1)S(1)} collective-permute-done((bf16[528,1024]{1,0:T(8,128)(2,1)S(1)}, bf16[528,1024]{1,0:T(8,128)(2,1)S(1)}, u32[]{:S(2)}, u32[]{:S(2)}) %collective-permute-start.8) | collective-permute-done | bytes 1081376 | tf_op jit(solution)/shard_map/ppermute | solution.py:373
  74.7 1.0 collective-permute-start.9
  75.7 9.2 %contribute.6.refs_4_ = f32[1024,1024]{1,0:T(8,128)S(1)} custom-call(s32[1]{0:T(128)} %bitcast.sign_ref, bf16[1024,1024]{1,0:T(8,128)(2,1)S(1)} %copy-done.1, bf16[528,1024]{1,0:T(8,128)(2,1)S(1)} %collective-permute-done.6.refs_0_, bf16[528,1024]{1,0:T(8,128)(2,1)S(1)} %collective-permute-done.7.refs_1_, ...), custom_call_target="tpu_custom_call", output_to_operand_aliasing={{}: (6, {})} | custom-call | flops 1048576 | bytes 65536 | tf_op jit(solution)/shard_map/contribute/pallas_call | solution.py:203
  84.9 1.0 collective-permute-done.11.refs_2_
  85.9 5.6 %collective-permute-start.15 = (bf16[512,1024]{1,0:T(8,128)(2,1)S(1)}, bf16[512,1024]{1,0:T(8,128)(2,1)S(1)}, u32[]{:S(2)}, u32[]{:S(2)}) collective-permute-start(bf16[512,1024]{1,0:T(8,128)(2,1)S(1)} %collective-permute-done.13.refs_3_), channel_id=1, source_target_pairs={{0,127},{1,2},{2,1},{3,4},{4,3},{5,6},{6,5},{7,8},{8,7},{9,10},{10... | collective-permute-start | bytes 3145736 | tf_op jit(solution)/shard_map/ppermute | solution.py:373
  91.5 7.7 %contribute.7.acc_ref = f32[1024,1024]{1,0:T(8,128)S(1)} custom-call(s32[1]{0:T(128)} %bitcast.sign_ref, bf16[1024,1024]{1,0:T(8,128)(2,1)S(1)} %copy-done.1, bf16[528,1024]{1,0:T(8,128)(2,1)S(1)} %collective-permute-done.8.refs_0_, bf16[528,1024]{1,0:T(8,128)(2,1)S(1)} %collective-permute-done.10.refs_1_, ...), custom_call_target="tpu_custom_call", output_to_operand_aliasing={{}: (6, {})} | custom-call | flops 1048576 | bytes 65536 | tf_op jit(solution)/shard_map/contribute/pallas_call | solution.py:203
  99.2 2.7 %gains.1.g_ref = bf16[1024,512]{1,0:T(8,128)(2,1)S(1)} custom-call(s32[1]{0:T(128)} %bitcast.sign_ref, bf16[1024,1024]{1,0:T(8,128)(2,1)S(1)} %copy-done.1, bf16[528,1024]{1,0:T(8,128)(2,1)S(1)} %collective-permute-done.9.a_ref), custom_call_target="tpu_custom_call" | custom-call | flops 1048576 | bytes 65536 | tf_op jit(solution)/shard_map/gains/pallas_call | solution.py:226
  102.0 6.8 %collective-permute-done.15.n_ref = bf16[512,1024]{1,0:T(8,128)(2,1)S(1)} collective-permute-done((bf16[512,1024]{1,0:T(8,128)(2,1)S(1)}, bf16[512,1024]{1,0:T(8,128)(2,1)S(1)}, u32[]{:S(2)}, u32[]{:S(2)}) %collective-permute-start.15) | collective-permute-done | bytes 1048608 | tf_op jit(solution)/shard_map/ppermute | solution.py:373
  108.8 3.0 %edges.1 = (f32[1024,1024]{1,0:T(8,128)S(1)}, bf16[256,1024]{1,0:T(8,128)(2,1)S(1)}, bf16[256,1024]{1,0:T(8,128)(2,1)S(1)}, bf16[512,1024]{1,0:T(8,128)(2,1)S(1)}) custom-call(s32[1]{0:T(128)} %bitcast.sign_ref, f32[1024,1024]{1,0:T(8,128)S(1)} %contribute.7.acc_ref, bf16[1024,512]{1,0:T(8,128)(2,1)S(1)} %gains.1.g_ref, ...), custom_call_target="tpu_custom_call", output_to_operand_aliasing={{0}: (1, {})} | custom-call | flops 1048576 | bytes 65536 | tf_op jit(solution)/shard_map/edges/pallas_call | solution.py:260
  111.8 2.5 %collective-permute-start.16 = (bf16[256,1024]{1,0:T(8,128)(2,1)S(1)}, bf16[256,1024]{1,0:T(8,128)(2,1)S(1)}, u32[]{:S(2)}, u32[]{:S(2)}) collective-permute-start(bf16[256,1024]{1,0:T(8,128)(2,1)S(1)} %get-tuple-element.48), channel_id=1, source_target_pairs={{0,127},{1,2},{2,1},{3,4},{4,3},{5,6},{6,5},{7,8},{8,7},{9,10},{10... | collective-permute-start | bytes 1572872 | tf_op jit(solution)/shard_map/ppermute | solution.py:373
  114.3 0.0 collective-permute-start.17
  114.3 2.6 %middle.1 = (f32[512,1024]{1,0:T(8,128)S(1)}, f32[1024,1024]{1,0:T(8,128)}) custom-call(f32[1024,1024]{1,0:T(8,128)S(1)} %get-tuple-element.45.acc_ref, bf16[1024,512]{1,0:T(8,128)(2,1)S(1)} %gains.1.g_ref, bf16[512,1024]{1,0:T(8,128)(2,1)S(1)} %get-tuple-element.46.w_ref), custom_call_target="tpu_custom_call" | custom-call | flops 1048576 | bytes 65536 | tf_op jit(solution)/shard_map/middle/pallas_call | solution.py:310
  116.9 9.0 %collective-permute-done.16.cross_ref = bf16[256,1024]{1,0:T(8,128)(2,1)S(1)} collective-permute-done((bf16[256,1024]{1,0:T(8,128)(2,1)S(1)}, bf16[256,1024]{1,0:T(8,128)(2,1)S(1)}, u32[]{:S(2)}, u32[]{:S(2)}) %collective-permute-start.16) | collective-permute-done | bytes 524320 | tf_op jit(solution)/shard_map/ppermute | solution.py:373
  125.9 2.2 %outer.1 = f32[1024,1024]{1,0:T(8,128)} custom-call(s32[1]{0:T(128)} %bitcast.sign_ref, f32[1024,1024]{1,0:T(8,128)S(1)} %get-tuple-element.45.acc_ref, f32[512,1024]{1,0:T(8,128)S(1)} %get-tuple-element.47.mid_ref, bf16[256,1024]{1,0:T(8,128)(2,1)S(1)} %collective-permute-done.16.cross_ref, ...), custom_call_target="tpu_custom_call", output_to_operand_aliasing={{}: (5, {})} | custom-call | flops 1048576 | bytes 65536 | tf_op jit(solution)/shard_map/outer/pallas_call | solution.py:349
  (22 shorter events, 0.1 us)
Async XLA Ops:
  1.8 20.9 %collective-permute-start.3 = (bf16[512,1024]{1,0:T(8,128)(2,1)S(1)}, bf16[512,1024]{1,0:T(8,128)(2,1)}, u32[]{:S(2)}, u32[]{:S(2)}) collective-permute-start(bf16[512,1024]{1,0:T(8,128)(2,1)S(1)} %convert_element_type.3.refs_2_), channel_id=1, source_target_pairs={{0,127},{1,2},{2,1},{3,4},{4,3},{5,6},{6,5},{7,8},{8,7},{9,10},{10... | collective-permute-start | bytes 3145736 | tf_op jit(solution)/shard_map/ppermute | solution.py:373
  17.4 5.2 %collective-permute-start.1 = (bf16[528,1024]{1,0:T(8,128)(2,1)}, bf16[528,1024]{1,0:T(8,128)(2,1)S(1)}, u32[]{:S(2)}, u32[]{:S(2)}) collective-permute-start(bf16[528,1024]{1,0:T(8,128)(2,1)} %get-tuple-element.29.refs_0_), channel_id=1, source_target_pairs={{0,1},{1,0},{2,3},{3,2},{4,5},{5,4},{6,7},{7,6},{8,9},{9,8},{10,11... | collective-permute-start | bytes 3244040 | tf_op jit(solution)/shard_map/ppermute | solution.py:372
  17.4 25.7 %collective-permute-start = (bf16[528,1024]{1,0:T(8,128)(2,1)}, bf16[528,1024]{1,0:T(8,128)(2,1)}, u32[]{:S(2)}, u32[]{:S(2)}) collective-permute-start(bf16[528,1024]{1,0:T(8,128)(2,1)} %get-tuple-element.29.refs_0_), channel_id=1, source_target_pairs={{0,127},{1,2},{2,1},{3,4},{4,3},{5,6},{6,5},{7,8},{8,7},{9,10},{10... | collective-permute-start | bytes 3244040 | tf_op jit(solution)/shard_map/ppermute | solution.py:373
  18.1 11.7 %collective-permute-start.2 = (bf16[512,1024]{1,0:T(8,128)(2,1)S(1)}, bf16[512,1024]{1,0:T(8,128)(2,1)}, u32[]{:S(2)}, u32[]{:S(2)}) collective-permute-start(bf16[512,1024]{1,0:T(8,128)(2,1)S(1)} %convert_element_type.3.refs_2_), channel_id=1, source_target_pairs={{0,1},{1,0},{2,3},{3,2},{4,5},{5,4},{6,7},{7,6},{8,9},{9,8},{10,11... | collective-permute-start | bytes 3145736 | tf_op jit(solution)/shard_map/ppermute | solution.py:372
  22.6 20.4 %collective-permute-start.4 = (bf16[512,1024]{1,0:T(8,128)(2,1)}, bf16[512,1024]{1,0:T(8,128)(2,1)}, u32[]{:S(2)}, u32[]{:S(2)}) collective-permute-start(bf16[512,1024]{1,0:T(8,128)(2,1)} %collective-permute-done.3.refs_2_), channel_id=1, source_target_pairs={{0,1},{1,0},{2,3},{3,2},{4,5},{5,4},{6,7},{7,6},{8,9},{9,8},{10,11... | collective-permute-start | bytes 3145736 | tf_op jit(solution)/shard_map/ppermute | solution.py:372
  22.6 26.6 %collective-permute-start.6 = (bf16[528,1024]{1,0:T(8,128)(2,1)S(1)}, bf16[528,1024]{1,0:T(8,128)(2,1)S(1)}, u32[]{:S(2)}, u32[]{:S(2)}) collective-permute-start(bf16[528,1024]{1,0:T(8,128)(2,1)S(1)} %collective-permute-done.1.refs_1_), channel_id=1, source_target_pairs={{0,127},{1,2},{2,1},{3,4},{4,3},{5,6},{6,5},{7,8},{8,7},{9,10},{10... | collective-permute-start | bytes 3244040 | tf_op jit(solution)/shard_map/ppermute | solution.py:373
  29.8 1.6 %copy-start = (bf16[1024,1024]{1,0:T(8,128)(2,1)S(1)}, bf16[1024,1024]{1,0:T(8,128)(2,1)}, u32[]{:S(2)}) copy-start(bf16[1024,1024]{1,0:T(8,128)(2,1)} %get-tuple-element.30.x_ref) | copy-start | bytes 6291460
  31.4 1.2 copy-start.3
  32.6 20.2 %copy-start.1 = (bf16[1024,1024]{1,0:T(8,128)(2,1)S(1)}, bf16[1024,1024]{1,0:T(8,128)(2,1)}, u32[]{:S(2)}) copy-start(bf16[1024,1024]{1,0:T(8,128)(2,1)} %get-tuple-element.30.x_ref) | copy-start | bytes 6291460
  32.6 20.2 %copy-start.2 = (f32[1024,1024]{1,0:T(8,128)S(1)}, f32[1024,1024]{1,0:T(8,128)}, u32[]{:S(2)}) copy-start(f32[1024,1024]{1,0:T(8,128)} %refs_5_.1) | copy-start | bytes 12582916
  43.1 6.2 %collective-permute-start.5 = (bf16[528,1024]{1,0:T(8,128)(2,1)}, bf16[528,1024]{1,0:T(8,128)(2,1)S(1)}, u32[]{:S(2)}, u32[]{:S(2)}) collective-permute-start(bf16[528,1024]{1,0:T(8,128)(2,1)} %collective-permute-done.refs_0_), channel_id=1, source_target_pairs={{0,1},{1,0},{2,3},{3,2},{4,5},{5,4},{6,7},{7,6},{8,9},{9,8},{10,11... | collective-permute-start | bytes 3244040 | tf_op jit(solution)/shard_map/ppermute | solution.py:372
  43.2 21.5 %collective-permute-start.12 = (bf16[512,1024]{1,0:T(8,128)(2,1)}, bf16[512,1024]{1,0:T(8,128)(2,1)S(1)}, u32[]{:S(2)}, u32[]{:S(2)}) collective-permute-start(bf16[512,1024]{1,0:T(8,128)(2,1)} %collective-permute-done.2.refs_3_), channel_id=1, source_target_pairs={{0,127},{1,2},{2,1},{3,4},{4,3},{5,6},{6,5},{7,8},{8,7},{9,10},{10... | collective-permute-start | bytes 3145736 | tf_op jit(solution)/shard_map/ppermute | solution.py:373
  49.3 19.2 %collective-permute-start.7 = (bf16[528,1024]{1,0:T(8,128)(2,1)S(1)}, bf16[528,1024]{1,0:T(8,128)(2,1)S(1)}, u32[]{:S(2)}, u32[]{:S(2)}) collective-permute-start(bf16[528,1024]{1,0:T(8,128)(2,1)S(1)} %collective-permute-done.6.refs_0_), channel_id=1, source_target_pairs={{0,1},{1,0},{2,3},{3,2},{4,5},{5,4},{6,7},{7,6},{8,9},{9,8},{10,11... | collective-permute-start | bytes 3244040 | tf_op jit(solution)/shard_map/ppermute | solution.py:372
  49.3 25.4 %collective-permute-start.8 = (bf16[528,1024]{1,0:T(8,128)(2,1)S(1)}, bf16[528,1024]{1,0:T(8,128)(2,1)S(1)}, u32[]{:S(2)}, u32[]{:S(2)}) collective-permute-start(bf16[528,1024]{1,0:T(8,128)(2,1)S(1)} %collective-permute-done.5.refs_1_), channel_id=1, source_target_pairs={{0,127},{1,2},{2,1},{3,4},{4,3},{5,6},{6,5},{7,8},{8,7},{9,10},{10... | collective-permute-start | bytes 3244040 | tf_op jit(solution)/shard_map/ppermute | solution.py:373
  64.7 11.0 %collective-permute-start.13 = (bf16[512,1024]{1,0:T(8,128)(2,1)S(1)}, bf16[512,1024]{1,0:T(8,128)(2,1)S(1)}, u32[]{:S(2)}, u32[]{:S(2)}) collective-permute-start(bf16[512,1024]{1,0:T(8,128)(2,1)S(1)} %collective-permute-done.12.refs_2_), channel_id=1, source_target_pairs={{0,1},{1,0},{2,3},{3,2},{4,5},{5,4},{6,7},{7,6},{8,9},{9,8},{10,11... | collective-permute-start | bytes 3145736 | tf_op jit(solution)/shard_map/ppermute | solution.py:372
  64.8 21.1 %collective-permute-start.11 = (bf16[512,1024]{1,0:T(8,128)(2,1)}, bf16[512,1024]{1,0:T(8,128)(2,1)S(1)}, u32[]{:S(2)}, u32[]{:S(2)}) collective-permute-start(bf16[512,1024]{1,0:T(8,128)(2,1)} %collective-permute-done.4.refs_3_), channel_id=1, source_target_pairs={{0,127},{1,2},{2,1},{3,4},{4,3},{5,6},{6,5},{7,8},{8,7},{9,10},{10... | collective-permute-start | bytes 3145736 | tf_op jit(solution)/shard_map/ppermute | solution.py:373
  74.7 16.8 %collective-permute-start.10 = (bf16[528,1024]{1,0:T(8,128)(2,1)S(1)}, bf16[528,1024]{1,0:T(8,128)(2,1)S(1)}, u32[]{:S(2)}, u32[]{:S(2)}) collective-permute-start(bf16[528,1024]{1,0:T(8,128)(2,1)S(1)} %collective-permute-done.8.refs_0_), channel_id=1, source_target_pairs={{0,1},{1,0},{2,3},{3,2},{4,5},{5,4},{6,7},{7,6},{8,9},{9,8},{10,11... | collective-permute-start | bytes 3244040 | tf_op jit(solution)/shard_map/ppermute | solution.py:372
  74.7 24.5 %collective-permute-start.9 = (bf16[528,1024]{1,0:T(8,128)(2,1)S(1)}, bf16[528,1024]{1,0:T(8,128)(2,1)S(1)}, u32[]{:S(2)}, u32[]{:S(2)}) collective-permute-start(bf16[528,1024]{1,0:T(8,128)(2,1)S(1)} %collective-permute-done.7.refs_1_), channel_id=1, source_target_pairs={{0,127},{1,2},{2,1},{3,4},{4,3},{5,6},{6,5},{7,8},{8,7},{9,10},{10... | collective-permute-start | bytes 3244040 | tf_op jit(solution)/shard_map/ppermute | solution.py:373
  85.9 5.6 %collective-permute-start.14 = (bf16[512,1024]{1,0:T(8,128)(2,1)S(1)}, bf16[512,1024]{1,0:T(8,128)(2,1)S(1)}, u32[]{:S(2)}, u32[]{:S(2)}) collective-permute-start(bf16[512,1024]{1,0:T(8,128)(2,1)S(1)} %collective-permute-done.11.refs_2_), channel_id=1, source_target_pairs={{0,1},{1,0},{2,3},{3,2},{4,5},{5,4},{6,7},{7,6},{8,9},{9,8},{10,11... | collective-permute-start | bytes 3145736 | tf_op jit(solution)/shard_map/ppermute | solution.py:372
  85.9 22.8 %collective-permute-start.15 = (bf16[512,1024]{1,0:T(8,128)(2,1)S(1)}, bf16[512,1024]{1,0:T(8,128)(2,1)S(1)}, u32[]{:S(2)}, u32[]{:S(2)}) collective-permute-start(bf16[512,1024]{1,0:T(8,128)(2,1)S(1)} %collective-permute-done.13.refs_3_), channel_id=1, source_target_pairs={{0,127},{1,2},{2,1},{3,4},{4,3},{5,6},{6,5},{7,8},{8,7},{9,10},{10... | collective-permute-start | bytes 3145736 | tf_op jit(solution)/shard_map/ppermute | solution.py:373
  111.8 14.1 %collective-permute-start.16 = (bf16[256,1024]{1,0:T(8,128)(2,1)S(1)}, bf16[256,1024]{1,0:T(8,128)(2,1)S(1)}, u32[]{:S(2)}, u32[]{:S(2)}) collective-permute-start(bf16[256,1024]{1,0:T(8,128)(2,1)S(1)} %get-tuple-element.48), channel_id=1, source_target_pairs={{0,127},{1,2},{2,1},{3,4},{4,3},{5,6},{6,5},{7,8},{8,7},{9,10},{10... | collective-permute-start | bytes 1572872 | tf_op jit(solution)/shard_map/ppermute | solution.py:373
  114.3 11.6 %collective-permute-start.17 = (bf16[256,1024]{1,0:T(8,128)(2,1)S(1)}, bf16[256,1024]{1,0:T(8,128)(2,1)S(1)}, u32[]{:S(2)}, u32[]{:S(2)}) collective-permute-start(bf16[256,1024]{1,0:T(8,128)(2,1)S(1)} %get-tuple-element.49), channel_id=1, source_target_pairs={{0,1},{1,0},{2,3},{3,2},{4,5},{5,4},{6,7},{7,6},{8,9},{9,8},{10,11... | collective-permute-start | bytes 1572872 | tf_op jit(solution)/shard_map/ppermute | solution.py:372
